TPU v7x, 32 devices: a whole 2x2x4 slice. The times are simulated.
32 devices in a mesh: section: 2 (over core), dp: 8 (over z, y), mp: 2 (over x).
Axes of the slice: x: 2, y: 2, z: 4, core: 2. Of those that a mesh axis runs over, the one named last changes fastest.
Arguments:
- states: bfloat16 [2, 16, 128, 2816], P('section', 'dp'), may hold values from -8 to 8
- injection: bfloat16 [16, 128, 2816], P('dp', None, 'mp'), may hold values from -2.390625 to 2.390625
- cotangent: bfloat16 [16, 128, 2816], P('dp', None, 'mp'), may hold values from -6 to 6
- gain: float32 [2816], P('mp'), may hold values from 0.5 to 1.5
- weight: bfloat16 [2816, 2816], P(None, 'mp'), may hold values from -0.109375 to 0.109375
- exits: int32 [16], P('dp'), may hold values from 1 to 2, as said below
- order: int32 [8, 2], P('dp'), may hold values from 0 to 1, each once within a row
Outputs:
- d_injection: float32 [16, 128, 2816], P('dp', None, 'mp')
- d_weight: float32 [2816, 2816], P(('section', 'dp'), 'mp')
- d_gain: float32 [2816], P('mp')
Inputs may be any that keep to these rules, and one draw needn't show every extreme that they name: `exits`: some micro-batch runs all 2 iterations and some only one. `order`: each row is a permutation of 0 .. 1.
All inputs are finite; a program needn't handle non-finite values.
Results may differ from a plain program's by a relative error of at most 0.0033.
Values may be sent and summed in bfloat16 or wider, within the bound.
No kernel may reach another device: no remote copies, remote signals or barrier semaphores. Data moves between devices by JAX's collectives and lax.ppermute only.
A program may use at most 128 MiB of HBM per device.

v0:
```python
import jax
import jax.numpy as jnp
from jax import lax
from jax.experimental import pallas as pl
from jax.experimental.pallas import tpu as pltpu
from jax.sharding import PartitionSpec as P

epsilon = 1e-06
f32, bf16 = jnp.float32, jnp.bfloat16
VMEM = pl.BlockSpec(memory_space=pltpu.VMEM)
SMEM = pl.BlockSpec(memory_space=pltpu.SMEM)
HBM = pl.BlockSpec(memory_space=pltpu.HBM)


def call(kernel, outs, ins, scratch=(), limit=24):
    shapes = [jax.ShapeDtypeStruct(shape, kind) for shape, kind in outs]
    specs, values = zip(*ins)
    return pl.pallas_call(
        kernel,
        out_shape=shapes,
        in_specs=list(specs),
        out_specs=[VMEM] * len(shapes),
        scratch_shapes=list(scratch),
        compiler_params=pltpu.CompilerParams(vmem_limit_bytes=limit * 2**20),
        cost_estimate=pl.CostEstimate(flops=1000, bytes_accessed=1000, transcendentals=0),
    )(*values)


def swap(value, axis):
    return lax.ppermute(value, axis, [(0, 1), (1, 0)])


def opposite(value):
    return lax.ppermute(value, ("section", "mp"), [(i, 3 - i) for i in range(4)])


def own_slot():
    return lax.axis_index("section") ^ lax.axis_index("mp")


def chunks_of(total, size):
    return [(start, min(size, total - start)) for start in range(0, total, size)]


def to_rows(columns):
    rows = columns[0].shape[0]
    lane = lax.broadcasted_iota(jnp.int32, (rows, 128), 1)
    wide = jnp.zeros((rows, 128), f32)
    for index, column in enumerate(columns):
        wide = jnp.where(lane == index, column, wide)
    return wide.T[:8]


def to_columns(packed):
    return jnp.concatenate([packed] * 16, axis=0).T


def load(stash, weight, chips, group):
    slots, rows, features = stash.shape
    block = features // (2 * chips)
    groups = chips // group
    height = 2 * groups * block
    parts = chunks_of(features, 512)

    def kernel(stash_hbm, weight_hbm, w, x, *refs):
        *out_refs, turned, sems = refs
        copy = pltpu.make_async_copy(stash_hbm, x, sems.at[len(parts)])
        copy.start()
        copies = []
        for index, (start, size) in enumerate(parts):
            part = pl.ds(start, size)
            copies.append(pltpu.make_async_copy(weight_hbm.at[part], w.at[part], sems.at[index]))
            copies[-1].start()
        copy.wait()
        turned[...] = x[own_slot()].T
        dp = lax.axis_index("dp")
        for distance, out_ref in enumerate(out_refs):
            for half in range(2):
                for other in range(groups):
                    chip = dp ^ (distance + group * other)
                    source = pl.multiple_of((half * chips + chip) * block, 16)
                    base = (half * groups + other) * block
                    out_ref[base : base + block] = turned[pl.ds(source, block)]
        for each in copies:
            each.wait()

    pieces = group if block % 16 == 0 else 0
    weight, loaded, *columns = call(
        kernel,
        [(weight.shape, bf16), (stash.shape, bf16)] + [((height, rows), bf16)] * pieces,
        [(HBM, stash), (HBM, weight)],
        [
            pltpu.VMEM((features, rows), bf16),
            pltpu.SemaphoreType.DMA((len(parts) + 1,)),
        ],
        limit=42,
    )
    if not columns:
        turned = lax.dynamic_index_in_dim(stash, own_slot(), 0, keepdims=False).T
        turned = turned.reshape(2, chips, block, rows)
        for distance in range(group):
            picked = [
                lax.dynamic_index_in_dim(
                    turned, lax.axis_index("dp") ^ (distance + group * other), 1, keepdims=False
                )
                for other in range(groups)
            ]
            columns.append(jnp.stack(picked, axis=1).reshape(height, rows))
    return weight, loaded, columns


def forward(stash, weight, injection, order):
    slots, rows, features = stash.shape
    half = weight.shape[1]

    def kernel(order_ref, stash_ref, weight_ref, inj_ref, keep_ref, send_ref, acc):
        slot = own_slot()
        left = stash_ref[...].reshape(slots * rows, features)
        for start, size in chunks_of(half, 512):
            part = slice(start, start + size)
            term = jnp.dot(left, weight_ref[:, part], preferred_element_type=f32)
            acc[:, :, part] = term.reshape(slots, rows, size)
        keep_ref[...] = acc[slot] + inj_ref[order_ref[0, slot]].astype(f32)
        send_ref[...] = acc[1 - slot] + inj_ref[order_ref[0, 1 - slot]].astype(f32)

    return call(
        kernel,
        [((rows, half), f32)] * 2,
        [(SMEM, order), (VMEM, stash), (VMEM, weight), (VMEM, injection)],
        [pltpu.VMEM((slots, rows, half), f32)],
    )


def row_sums(order, cotangent, gain, keep, got):
    rows = keep.shape[0]

    def kernel(order_ref, cot_ref, gain_ref, keep_ref, got_ref, out_ref):
        sec = lax.axis_index("section")
        first = sec == 0
        keep, got = keep_ref[...], got_ref[...]
        pre1, pre0 = jnp.where(first, got, keep), jnp.where(first, keep, got)
        u = cot_ref[order_ref[0, own_slot()]].astype(f32) * gain_ref[...]
        sums = [pre1 * pre1, u * pre1, pre0 * pre0]
        out_ref[...] = to_rows([jnp.sum(each, axis=1, keepdims=True) for each in sums])

    ins = [(SMEM, order), (VMEM, cotangent), (VMEM, gain), (VMEM, keep), (VMEM, got)]
    return call(kernel, [((8, rows), f32)], ins)[0]


def delta_of(pre, u, squares, inner, features):
    radius = jnp.sqrt(squares / features + epsilon)
    inverse = 1.0 / radius
    normed = pre * inverse
    return normed, (u - normed * (inner * inverse / features)) * inverse


def lower_iteration1(order, exits, cotangent, gain, keep, got, sums, others, weight):
    rows, half = keep.shape
    features = weight.shape[0]

    def kernel(order_ref, exits_ref, cot_ref, gain_ref, keep_ref, got_ref, sums_ref, others_ref,
               weight_ref, db_ref, delta_ref, gain_out, away_ref):
        sec, mp = lax.axis_index("section"), lax.axis_index("mp")
        micro = order_ref[0, own_slot()]
        live = jnp.where(exits_ref[micro] > 1, 1.0, 0.0)
        stats = to_columns(sums_ref[...] + others_ref[...])
        pre = jnp.where(sec == 0, got_ref[...], keep_ref[...])
        cot = cot_ref[micro].astype(f32)
        normed, delta = delta_of(pre, cot * gain_ref[...], stats[:, 0:1], stats[:, 1:2], features)
        delta = delta * live
        delta_ref[...] = delta
        db = delta.astype(bf16)
        db_ref[...] = db
        gain_out[...] = jnp.sum(cot * normed, axis=0, keepdims=True) * live
        part = weight_ref[pl.ds(pl.multiple_of((1 - mp) * half, 128), half)]
        away_ref[...] = lax.dot_general(
            part, db, (((1,), (1,)), ((), ())), preferred_element_type=f32
        ).astype(bf16)

    return call(
        kernel,
        [((rows, half), bf16), ((rows, half), f32), ((1, half), f32), ((half, rows), bf16)],
        [(SMEM, order), (SMEM, exits), (VMEM, cotangent), (VMEM, gain), (VMEM, keep), (VMEM, got),
         (VMEM, sums), (VMEM, others), (VMEM, weight)],
    )


def kept_half(db, weight):
    rows, half = db.shape

    def kernel(db_ref, weight_ref, out_ref):
        part = weight_ref[pl.ds(pl.multiple_of(lax.axis_index("mp") * half, 128), half)]
        out_ref[...] = lax.dot_general(
            part, db_ref[...], (((1,), (1,)), ((), ())), preferred_element_type=f32
        )

    return call(kernel, [((half, rows), f32)], [(VMEM, db), (VMEM, weight)])[0]


def carry(order, exits, cotangent, gain, keep, got, sums, others, kept, sent, gain1, features):
    rows, half = keep.shape

    def kernel(order_ref, exits_ref, cot_ref, gain_ref, keep_ref, got_ref, sums_ref, others_ref,
               kept_ref, sent_ref, gain1_ref, carried_ref, inner_ref, gain_out):
        sec = lax.axis_index("section")
        micro = order_ref[0, own_slot()]
        passed = (kept_ref[...] + sent_ref[...].astype(f32)).astype(bf16).astype(f32).T
        cot = cot_ref[micro].astype(f32)
        carried = jnp.where(exits_ref[micro] > 1, passed, cot)
        carried_ref[...] = carried
        pre = jnp.where(sec == 0, keep_ref[...], got_ref[...])
        inner = jnp.sum(carried * gain_ref[...] * pre, axis=1, keepdims=True)
        inner_ref[...] = to_rows([inner])
        squares = to_columns(sums_ref[...] + others_ref[...])[:, 2:3]
        inverse = 1.0 / jnp.sqrt(squares / features + epsilon)
        gains = jnp.sum(carried * (pre * inverse), axis=0, keepdims=True) + gain1_ref[...]
        gain_out[...] = jnp.broadcast_to(gains, (8, half))

    return call(
        kernel,
        [((rows, half), f32), ((8, rows), f32), ((8, half), f32)],
        [(SMEM, order), (SMEM, exits)]
        + [
            (VMEM, value)
            for value in (cotangent, gain, keep, got, sums, others, kept, sent, gain1)
        ],
    )


def iteration0(gain, keep, got, sums, others, carried, inner, inner_other, delta1, features):
    rows, half = keep.shape

    def kernel(gain_ref, keep_ref, got_ref, sums_ref, others_ref, carried_ref, inner_ref, other_ref,
               delta1_ref, total_ref, db_ref):
        sec = lax.axis_index("section")
        squares = to_columns(sums_ref[...] + others_ref[...])[:, 2:3]
        inner = to_columns(inner_ref[...] + other_ref[...])[:, 0:1]
        pre = jnp.where(sec == 0, keep_ref[...], got_ref[...])
        _, delta = delta_of(pre, carried_ref[...] * gain_ref[...], squares, inner, features)
        total_ref[...] = delta + delta1_ref[...]
        db_ref[...] = delta.astype(bf16)

    values = [gain, keep, got, sums, others, carried, inner, inner_other, delta1]
    return call(
        kernel,
        [((rows, half), f32), ((rows, half), bf16)],
        [(VMEM, value) for value in values],
    )


def stacked(columns):
    def kernel(*refs):
        for chip, ref in enumerate(refs[:-1]):
            refs[-1][chip] = ref[...]

    outs = [((len(columns), *columns[0].shape), bf16)]
    return call(kernel, outs, [(VMEM, value) for value in columns])[0]


def left_side(columns, others):
    group, height, rows = columns.shape

    def kernel(own_ref, other_ref, out_ref):
        for index, pair in enumerate([(own_ref, other_ref), (other_ref, own_ref)]):

            @pl.when(lax.axis_index("section") == index)
            def _():
                for k, ref in enumerate(pair):
                    for chip in range(group):
                        base = (k * group + chip) * rows
                        out_ref[:, base : base + rows] = ref[chip]

    return call(
        kernel,
        [((height, 2 * group * rows), bf16)],
        [(VMEM, value) for value in (columns, others)],
    )[0]


def weight_terms(left, grads, lanes):
    rows = grads[0].shape[0]
    height = left.shape[0]
    start, width = lanes

    def kernel(left_ref, *refs):
        grads_refs, (keep_ref, send_ref, right) = refs[:-3], refs[-3:]
        for index, grads_ref in enumerate(grads_refs):
            right[index * rows : (index + 1) * rows] = grads_ref[:, start : start + width]
        for k, (first, second) in enumerate([(keep_ref, send_ref), (send_ref, keep_ref)]):

            @pl.when(lax.axis_index("section") == k)
            def _():
                terms = jnp.dot(left_ref[...], right[...], preferred_element_type=f32)
                first[...] = terms[: height // 2]
                second[...] = terms[height // 2 :]

    return call(
        kernel,
        [((height // 2, width), f32)] * 2,
        [(VMEM, value) for value in [left, *grads]],
        [pltpu.VMEM((len(grads) * rows, width), bf16)],
    )


def chip_sum(keep, other, block, gains=()):
    height, width = keep.shape
    extra = 16 if gains else 0

    def kernel(keep_ref, other_ref, *refs):
        gain_refs, (own_ref, *away_refs) = refs[: len(gains)], refs[len(gains) :]
        total = keep_ref[...] + other_ref[...]
        own_ref[...] = total[:block]
        for index, away_ref in enumerate(away_refs):
            away_ref[:block] = total[(index + 1) * block : (index + 2) * block].astype(bf16)
        if gains:
            rest = group_gains(gain_refs)
            half = rest.shape[1]
            packed = []
            for _ in range(3):
                high = rest.astype(bf16).astype(f32)
                rest = rest - high
                tail = high[:, half - width :]
                packed += [high[:, :width], tail]
            packed.append(jnp.zeros((extra - len(packed), width), f32))
            for away_ref in away_refs:
                away_ref[block:] = jnp.concatenate(packed, axis=0).astype(bf16)

    outs = [((block, width), f32)] + [((block + extra, width), bf16)] * (height // block - 1)
    return call(kernel, outs, [(VMEM, value) for value in (keep, other, *gains)])


def group_gains(refs):
    return refs[0][:1] + refs[1][:1]


def final_sum(own, others, gains, half):
    block, first_width = own[0].shape
    count = len(others[0])

    def kernel(*refs):
        gain_refs, refs = refs[: len(gains)], refs[len(gains) :]
        weight_out, gain_out = refs[-2:]
        start = 0
        for part in range(len(own)):
            own_ref, *other_refs = refs[part * (count + 1) : (part + 1) * (count + 1)]
            total = own_ref[...]
            for other_ref in other_refs:
                total = total + other_ref[:block].astype(f32)
            width = own_ref.shape[1]
            weight_out[:, start : start + width] = total
            start += width
        sums = [group_gains(gain_refs)]
        for ref in refs[1 : count + 1]:
            packed = ref[block:].astype(f32)
            heads = packed[0:1] + packed[2:3] + packed[4:5]
            tails = packed[1:2] + packed[3:4] + packed[5:6]
            tails = tails[:, 2 * first_width - half :]
            sums.append(jnp.concatenate([heads, tails], axis=1))
        while len(sums) > 1:
            sums = [a + b for a, b in zip(sums[::2], sums[1::2])]
        gain_out[...] = sums[0]

    values = [value for mine, theirs in zip(own, others) for value in (mine, *theirs)]
    ins = [(VMEM, value) for value in (*gains, *values)]
    return call(kernel, [((block, half), f32), ((1, half), f32)], ins)


def place(order, total, other):
    rows, half = total.shape

    def kernel(order_ref, total_ref, other_ref, out_ref):
        micro = order_ref[0, own_slot()]
        out_ref[micro] = total_ref[...]
        out_ref[1 - micro] = other_ref[...]

    ins = [(SMEM, order), (VMEM, total), (VMEM, other)]
    return call(kernel, [((2, rows, half), f32)], ins)[0]


def shards(states, injection, cotangent, gain, weight, exits, order):
    stash = states[0]
    slots, rows, features = stash.shape
    half = weight.shape[1]
    dp = lax.axis_index("dp")
    chips = lax.axis_size("dp")
    group = 4
    groups = chips // group
    assert slots == 2 and lax.axis_size("section") == 2 and lax.axis_size("mp") == 2
    assert chips % group == 0 and groups & (groups - 1) == 0

    def across(value, distance):
        return lax.ppermute(value, "dp", [(i, i ^ distance) for i in range(chips)])

    def gathered(value):
        return [value] + [across(value, distance) for distance in range(1, group)]

    block = features // (2 * chips)
    weight, stash, columns = load(stash, weight, chips, group)
    columns = columns[:1] + [across(columns[distance], distance) for distance in range(1, group)]

    gain = gain.reshape(1, half)
    keep, send = forward(stash, weight, injection, order)
    got = swap(send, "section")
    sums = row_sums(order, cotangent, gain, keep, got)
    others = opposite(sums)
    others, columns = lax.optimization_barrier((others, columns))
    db1, delta1, gain1, away = lower_iteration1(
        order, exits, cotangent, gain, keep, got, sums, others, weight
    )
    sent = opposite(away)
    grads1 = gathered(db1)
    kept = kept_half(db1, weight)
    kept, sent = lax.optimization_barrier((kept, sent))

    carried, inner, gains = carry(
        order, exits, cotangent, gain, keep, got, sums, others, kept, sent, gain1, features
    )
    inner_other, gains_other = opposite(inner), swap(gains, "section")
    columns = stacked(columns)
    gains = gains + gains_other
    near_gains = across(gains, 1)
    inner_other, near_gains, columns, *grads1[1:] = lax.optimization_barrier(
        (inner_other, near_gains, columns, *grads1[1:])
    )
    total, db0 = iteration0(
        gain, keep, got, sums, others, carried, inner, inner_other, delta1, features
    )
    grads0 = gathered(db0)
    columns, total = lax.optimization_barrier((columns, total))
    left = left_side(columns, opposite(columns))

    gains = gains + near_gains
    gains = [gains, across(gains, 2)]
    left, grads0, gains = lax.optimization_barrier((left, grads0, gains))

    cut = (half * 9 // 16 + 127) // 128 * 128
    terms = [
        weight_terms(left, grads0 + grads1, lanes) for lanes in [(0, cut), (cut, half - cut)]
    ]
    arrived = [swap(send, "section") for _, send in terms]
    own, others = [], []
    for part, (keep, _) in enumerate(terms):
        if part:
            keep, *_ = lax.optimization_barrier((keep, *aways))
            total, *_ = lax.optimization_barrier((total, *aways))
        mine, *aways = chip_sum(keep, arrived[part], block, () if part else gains)
        own.append(mine)
        others.append([across(away, group * (i + 1)) for i, away in enumerate(aways)])
    d_injection = place(order, total, swap(total, "section"))
    others[1], d_injection = lax.optimization_barrier((others[1], d_injection))
    d_weight, d_gain = final_sum(own, others, gains, half)
    return (d_injection, d_weight, d_gain[0])


def solution(mesh):
    return jax.shard_map(
        shards,
        mesh=mesh,
        in_specs=(
            P("section", "dp", None, None),
            P("dp", None, "mp"),
            P("dp", None, "mp"),
            P("mp"),
            P(None, "mp"),
            P("dp"),
            P("dp", None),
        ),
        out_specs=(P("dp", None, "mp"), P(("section", "dp"), "mp"), P("mp")),
        check_vma=False,
    )
```

profile of v0, /device:TPU:0, one launch (start us, length us, event | category | flops | bytes accessed | tf_op | source)
XLA Modules:
  0.0 100.3 jit_solution(12390760002610683946)
XLA Ops:
  0.6 0.0 copy-start.1
  0.6 1.4 %copy-done.1 = bf16[1,2,128,2816]{3,2,1,0:T(8,128)(2,1)S(1)} copy-done((bf16[1,2,128,2816]{3,2,1,0:T(8,128)(2,1)S(1)}, bf16[1,2,128,2816]{3,2,1,0:T(8,128)(2,1)}, u32[]{:S(2)}) %copy-start.1) | copy-done | bytes 1441816
  2.0 3.6 %shard_map.94 = (bf16[2816,1408]{1,0:T(8,128)(2,1)S(1)}, bf16[2,128,2816]{2,1,0:T(8,128)(2,1)S(1)}, bf16[704,128]{1,0:T(8,128)(2,1)S(1)}, bf16[704,128]{1,0:T(8,...) custom-call(bf16[2,128,2816]{2,1,0:T(8,128)(2,1)S(1)} %bitcast.1, bf16[2816,1408]{1,0:T(8,128)(2,1)} %weight_hbm.1), custom_call_target="tpu_custom_call" | custom-call | flops 1000 | bytes 1000 | tf_op jit(solution)/shard_map/pallas_call | solution.py:18
  5.6 0.0 copy-start.5
  5.6 0.0 copy-start
  5.6 3.1 %shard_map.95 = (f32[128,1408]{1,0:T(8,128)S(1)}, f32[128,1408]{1,0:T(8,128)S(1)}) custom-call(s32[1,2]{1,0:T(1,128)S(1)} %copy-done.3, bf16[2,128,2816]{2,1,0:T(8,128)(2,1)S(1)} %get-tuple-element.56.stash_ref, bf16[2816,1408]{1,0:T(8,128)(2,1)S(1)} %get-tuple-element.57.weight_ref, bf16[2,128,1408]{2,1,0:T(8,128)(2,1)S(1)} %copy-done.2), custom_call_target="tpu_custom_call" | custom-call | flops 1000 | bytes 1000 | tf_op jit(solution)/shard_map/pallas_call | solution.py:18
  8.7 0.0 copy-start.4
  8.7 0.5 collective-permute-start
  9.2 2.6 %collective-permute-start.2 = (bf16[704,128]{1,0:T(8,128)(2,1)S(1)}, bf16[704,128]{1,0:T(8,128)(2,1)S(1)}, u32[]{:S(2)}, u32[]{:S(2)}) collective-permute-start(bf16[704,128]{1,0:T(8,128)(2,1)S(1)} %get-tuple-element.61), channel_id=1, source_target_pairs={{0,2},{2,0},{4,6},{6,4},{8,10},{10,8},{12,14},{14,12},{1,3},{3,1},... | collective-permute-start | bytes 540680 | tf_op jit(solution)/shard_map/ppermute | solution.py:392
  11.8 1.6 %collective-permute-start.3 = (bf16[704,128]{1,0:T(8,128)(2,1)S(1)}, bf16[704,128]{1,0:T(8,128)(2,1)S(1)}, u32[]{:S(2)}, u32[]{:S(2)}) collective-permute-start(bf16[704,128]{1,0:T(8,128)(2,1)S(1)} %get-tuple-element.62), channel_id=1, source_target_pairs={{0,4},{2,6},{4,0},{6,2},{8,12},{10,14},{12,8},{14,10},{1,5},{3,7},... | collective-permute-start | bytes 540680 | tf_op jit(solution)/shard_map/ppermute | solution.py:392
  13.4 0.0 collective-permute-start.4
  13.4 0.0 collective-permute-done.got_ref
  13.4 0.9 shard_map.96.sums_ref
  14.3 1.1 %collective-permute-start.1 = (f32[8,128]{1,0:T(8,128)S(1)}, f32[8,128]{1,0:T(8,128)S(1)}, u32[]{:S(2)}, u32[]{:S(2)}) collective-permute-start(f32[8,128]{1,0:T(8,128)S(1)} %shard_map.96.sums_ref), channel_id=1, source_target_pairs={{0,17},{1,16},{16,1},{17,0},{2,19},{3,18},{18,3},{19,2},{4,21},{5,... | collective-permute-start | bytes 12296 | tf_op jit(solution)/shard_map/ppermute | solution.py:34
  15.4 1.5 %collective-permute-done.2.refs_1_ = bf16[704,128]{1,0:T(8,128)(2,1)S(1)} collective-permute-done((bf16[704,128]{1,0:T(8,128)(2,1)S(1)}, bf16[704,128]{1,0:T(8,128)(2,1)S(1)}, u32[]{:S(2)}, u32[]{:S(2)}) %collective-permute-start.2) | collective-permute-done | bytes 180256 | tf_op jit(solution)/shard_map/ppermute | solution.py:392
  17.0 2.3 %collective-permute-done.3.refs_2_ = bf16[704,128]{1,0:T(8,128)(2,1)S(1)} collective-permute-done((bf16[704,128]{1,0:T(8,128)(2,1)S(1)}, bf16[704,128]{1,0:T(8,128)(2,1)S(1)}, u32[]{:S(2)}, u32[]{:S(2)}) %collective-permute-start.3) | collective-permute-done | bytes 180256 | tf_op jit(solution)/shard_map/ppermute | solution.py:392
  19.2 2.9 %collective-permute-done.4.refs_3_ = bf16[704,128]{1,0:T(8,128)(2,1)S(1)} collective-permute-done((bf16[704,128]{1,0:T(8,128)(2,1)S(1)}, bf16[704,128]{1,0:T(8,128)(2,1)S(1)}, u32[]{:S(2)}, u32[]{:S(2)}) %collective-permute-start.4) | collective-permute-done | bytes 180256 | tf_op jit(solution)/shard_map/ppermute | solution.py:392
  22.1 0.0 collective-permute-done.1.others_ref
  22.1 2.1 %shard_map.97 = (bf16[128,1408]{1,0:T(8,128)(2,1)S(1)}, f32[128,1408]{1,0:T(8,128)S(1)}, f32[1,1408]{1,0:T(1,128)S(1)}, bf16[1408,128]{1,0:T(8,128)(2,1)S(1)}) custom-call(s32[1,2]{1,0:T(1,128)S(1)} %copy-done.3, s32[2]{0:T(128)S(1)} %copy-done.4, bf16[2,128,1408]{2,1,0:T(8,128)(2,1)S(1)} %copy-done, f32[1,1408]{1,0:T(1,128)S(1)} %reshape.9.gain_ref, ...), custom_call_target="tpu_custom_call" | custom-call | flops 1000 | bytes 1000 | tf_op jit(solution)/shard_map/pallas_call | solution.py:18
  24.1 0.7 collective-permute-start.5
  24.8 2.5 %collective-permute-start.11 = (bf16[128,1408]{1,0:T(8,128)(2,1)S(1)}, bf16[128,1408]{1,0:T(8,128)(2,1)S(1)}, u32[]{:S(2)}, u32[]{:S(2)}) collective-permute-start(bf16[128,1408]{1,0:T(8,128)(2,1)S(1)} %get-tuple-element.65.db_ref.refs_4_), channel_id=1, source_target_pairs={{0,6},{2,4},{4,2},{6,0},{8,14},{10,12},{12,10},{14,8},{1,7},{3,5},... | collective-permute-start | bytes 1081352 | tf_op jit(solution)/shard_map/ppermute | solution.py:392
  27.3 0.4 collective-permute-start.10
  27.8 0.5 collective-permute-start.9
  28.3 1.2 %shard_map.98.kept_ref = f32[1408,128]{1,0:T(8,128)S(1)} custom-call(bf16[128,1408]{1,0:T(8,128)(2,1)S(1)} %get-tuple-element.65.db_ref.refs_4_, bf16[2816,1408]{1,0:T(8,128)(2,1)S(1)} %get-tuple-element.57.weight_ref), custom_call_target="tpu_custom_call" | custom-call | flops 1000 | bytes 1000 | tf_op jit(solution)/shard_map/pallas_call | solution.py:18
  29.5 5.2 %collective-permute-done.5.sent_ref = bf16[1408,128]{1,0:T(8,128)(2,1)S(1)} collective-permute-done((bf16[1408,128]{1,0:T(8,128)(2,1)S(1)}, bf16[1408,128]{1,0:T(8,128)(2,1)S(1)}, u32[]{:S(2)}, u32[]{:S(2)}) %collective-permute-start.5) | collective-permute-done | bytes 360480 | tf_op jit(solution)/shard_map/ppermute | solution.py:34
  34.7 1.0 %shard_map.99 = (f32[128,1408]{1,0:T(8,128)S(1)}, f32[8,128]{1,0:T(8,128)S(1)}, f32[8,1408]{1,0:T(8,128)S(1)}) custom-call(s32[1,2]{1,0:T(1,128)S(1)} %copy-done.3, s32[2]{0:T(128)S(1)} %copy-done.4, bf16[2,128,1408]{2,1,0:T(8,128)(2,1)S(1)} %copy-done, f32[1,1408]{1,0:T(1,128)S(1)} %reshape.9.gain_ref, f32[128,1408]{1,0:T(8,128)S(1)} %get-tuple-element.58.keep_ref, ...), custom_call_target="tpu_custom_call" | custom-call | flops 1000 | bytes 1000 | tf_op jit(solution)/shard_map/pallas_call | solution.py:18
  35.7 0.4 collective-permute-start.7
  36.1 0.9 collective-permute-done.7
  37.0 1.9 %collective-permute-start.8 = (f32[8,1408]{1,0:T(8,128)S(1)}, f32[8,1408]{1,0:T(8,128)S(1)}, u32[]{:S(2)}, u32[]{:S(2)}) collective-permute-start(f32[8,1408]{1,0:T(8,128)S(1)} %add.6), channel_id=1, source_target_pairs={{0,2},{2,0},{4,6},{6,4},{8,10},{10,8},{12,14},{14,12},{1,3},{3,1},... | collective-permute-start | bytes 135176 | tf_op jit(solution)/shard_map/ppermute | solution.py:392
  38.9 0.5 collective-permute-start.6
  39.5 0.0 collective-permute-done.11.refs_7_
  39.5 5.1 %collective-permute-done.10.refs_6_ = bf16[128,1408]{1,0:T(8,128)(2,1)S(1)} collective-permute-done((bf16[128,1408]{1,0:T(8,128)(2,1)S(1)}, bf16[128,1408]{1,0:T(8,128)(2,1)S(1)}, u32[]{:S(2)}, u32[]{:S(2)}) %collective-permute-start.10) | collective-permute-done | bytes 360480 | tf_op jit(solution)/shard_map/ppermute | solution.py:392
  44.6 0.1 collective-permute-done.9.refs_5_
  44.8 0.0 collective-permute-done.6.other_ref
  44.8 0.9 collective-permute-done.8
  45.7 0.4 shard_map.101
  46.1 0.3 collective-permute-start.12
  46.5 2.6 %collective-permute-start.15 = (bf16[128,1408]{1,0:T(8,128)(2,1)S(1)}, bf16[128,1408]{1,0:T(8,128)(2,1)S(1)}, u32[]{:S(2)}, u32[]{:S(2)}) collective-permute-start(bf16[128,1408]{1,0:T(8,128)(2,1)S(1)} %get-tuple-element.85.refs_0_), channel_id=1, source_target_pairs={{0,6},{2,4},{4,2},{6,0},{8,14},{10,12},{12,10},{14,8},{1,7},{3,5},... | collective-permute-start | bytes 1081352 | tf_op jit(solution)/shard_map/ppermute | solution.py:392
  49.1 0.4 collective-permute-start.14
  49.6 0.4 collective-permute-start.13
  50.0 1.7 %collective-permute-start.16 = (f32[8,1408]{1,0:T(8,128)S(1)}, f32[8,1408]{1,0:T(8,128)S(1)}, u32[]{:S(2)}, u32[]{:S(2)}) collective-permute-start(f32[8,1408]{1,0:T(8,128)S(1)} %add.7.refs_0_), channel_id=1, source_target_pairs={{0,4},{2,6},{4,0},{6,2},{8,12},{10,14},{12,8},{14,10},{1,5},{3,7},... | collective-permute-start | bytes 135176 | tf_op jit(solution)/shard_map/ppermute | solution.py:392
  51.7 12.7 %collective-permute-done.12.other_ref = bf16[4,704,128]{2,1,0:T(8,128)(2,1)S(1)} collective-permute-done((bf16[4,704,128]{2,1,0:T(8,128)(2,1)S(1)}, bf16[4,704,128]{2,1,0:T(8,128)(2,1)S(1)}, u32[]{:S(2)}, u32[]{:S(2)}) %collective-permute-start.12) | collective-permute-done | bytes 720928 | tf_op jit(solution)/shard_map/ppermute | solution.py:34
  64.4 0.4 shard_map.102.left_ref
  64.8 2.3 %collective-permute-done.16.refs_1_ = f32[8,1408]{1,0:T(8,128)S(1)} collective-permute-done((f32[8,1408]{1,0:T(8,128)S(1)}, f32[8,1408]{1,0:T(8,128)S(1)}, u32[]{:S(2)}, u32[]{:S(2)}) %collective-permute-start.16) | collective-permute-done | bytes 45088 | tf_op jit(solution)/shard_map/ppermute | solution.py:392
  67.1 0.0 collective-permute-done.15.refs_3_
  67.1 0.0 collective-permute-done.14.refs_2_
  67.1 0.0 collective-permute-done.13.refs_1_
  67.1 1.8 %shard_map.104 = (f32[352,896]{1,0:T(8,128)S(1)}, f32[352,896]{1,0:T(8,128)S(1)}) custom-call(bf16[704,1024]{1,0:T(8,128)(2,1)S(1)} %shard_map.102.left_ref, bf16[128,1408]{1,0:T(8,128)(2,1)S(1)} %get-tuple-element.85.refs_0_, bf16[128,1408]{1,0:T(8,128)(2,1)S(1)} %collective-permute-done.13.refs_1_, bf16[128,1408]{1,0:T(8,128)(2,1)S(1)} %collective-permute-done.14.refs_2_, ...), custom_call_target="tpu_custom_call" | custom-call | flops 1000 | bytes 1000 | tf_op jit(solution)/shard_map/pallas_call | solution.py:18
  68.9 0.1 collective-permute-start.17
  69.0 1.0 shard_map.103
  69.9 0.6 collective-permute-start.18
  70.5 1.4 %collective-permute-done.17.other_ref = f32[352,896]{1,0:T(8,128)S(1)} collective-permute-done((f32[352,896]{1,0:T(8,128)S(1)}, f32[352,896]{1,0:T(8,128)S(1)}, u32[]{:S(2)}, u32[]{:S(2)}) %collective-permute-start.17) | collective-permute-done | bytes 1261600 | tf_op jit(solution)/shard_map/ppermute | solution.py:30
  71.9 0.2 shard_map.105
  72.1 0.2 collective-permute-start.20
  72.3 2.6 %collective-permute-start.21 = (bf16[192,896]{1,0:T(8,128)(2,1)S(1)}, bf16[192,896]{1,0:T(8,128)(2,1)S(1)}, u32[]{:S(2)}, u32[]{:S(2)}) collective-permute-start(bf16[192,896]{1,0:T(8,128)(2,1)S(1)} %get-tuple-element.97), channel_id=1, source_target_pairs={{0,8},{2,10},{4,12},{6,14},{8,0},{10,2},{12,4},{14,6},{1,9},{3,11}... | collective-permute-start | bytes 1032200 | tf_op jit(solution)/shard_map/ppermute | solution.py:392
  74.9 0.0 collective-permute-done.18.other_ref
  74.9 0.1 shard_map.106
  75.0 0.7 collective-permute-start.19
  75.7 0.0 collective-permute-done.20.other_ref
  75.7 1.7 %shard_map.107 = f32[2,128,1408]{2,1,0:T(8,128)} custom-call(s32[1,2]{1,0:T(1,128)S(1)} %copy-done.3, f32[128,1408]{1,0:T(8,128)S(1)} %get-tuple-element.102.total_ref, f32[128,1408]{1,0:T(8,128)S(1)} %collective-permute-done.20.other_ref), custom_call_target="tpu_custom_call" | custom-call | flops 1000 | bytes 1000 | tf_op jit(solution)/shard_map/pallas_call | solution.py:18
  77.4 21.2 %collective-permute-done.19.refs_5_ = bf16[176,512]{1,0:T(8,128)(2,1)S(1)} collective-permute-done((bf16[176,512]{1,0:T(8,128)(2,1)S(1)}, bf16[176,512]{1,0:T(8,128)(2,1)S(1)}, u32[]{:S(2)}, u32[]{:S(2)}) %collective-permute-start.19) | collective-permute-done | bytes 180256 | tf_op jit(solution)/shard_map/ppermute | solution.py:392
  98.6 0.0 collective-permute-done.21.refs_3_
  98.6 1.0 %shard_map.108 = (f32[176,1408]{1,0:T(8,128)}, f32[1,1408]{1,0:T(1,128)S(1)}) custom-call(f32[8,1408]{1,0:T(8,128)S(1)} %add.7.refs_0_, f32[8,1408]{1,0:T(8,128)S(1)} %collective-permute-done.16.refs_1_, f32[176,896]{1,0:T(8,128)S(1)} %get-tuple-element.104.refs_2_, bf16[192,896]{1,0:T(8,128)(2,1)S(1)} %collective-permute-done.21.refs_3_, ...), custom_call_target="tpu_custom_call" | custom-call | flops 1000 | bytes 1000 | tf_op jit(solution)/shard_map/pallas_call | solution.py:18
  99.7 0.6 reduce
  (11 shorter events, 0.1 us)
Async XLA Ops:
  0.6 1.4 %copy-start.1 = (bf16[1,2,128,2816]{3,2,1,0:T(8,128)(2,1)S(1)}, bf16[1,2,128,2816]{3,2,1,0:T(8,128)(2,1)}, u32[]{:S(2)}) copy-start(bf16[1,2,128,2816]{3,2,1,0:T(8,128)(2,1)} %param.7) | copy-start | bytes 4325380
  2.0 3.6 %copy-start.2 = (bf16[2,128,1408]{2,1,0:T(8,128)(2,1)S(1)}, bf16[2,128,1408]{2,1,0:T(8,128)(2,1)}, u32[]{:S(2)}) copy-start(bf16[2,128,1408]{2,1,0:T(8,128)(2,1)} %inj_ref.1) | copy-start | bytes 2162692
  2.0 3.6 %copy-start.3 = (s32[1,2]{1,0:T(1,128)S(1)}, s32[1,2]{1,0:T(1,128)}, u32[]{:S(2)}) copy-start(s32[1,2]{1,0:T(1,128)} %order_ref.9) | copy-start | bytes 28
  5.6 7.8 %copy-start.5 = (f32[1408]{0:T(1024)S(1)}, f32[1408]{0:T(1024)}, u32[]{:S(2)}) copy-start(f32[1408]{0:T(1024)} %param.10) | copy-start | bytes 16900
  5.6 7.8 %copy-start = (bf16[2,128,1408]{2,1,0:T(8,128)(2,1)S(1)}, bf16[2,128,1408]{2,1,0:T(8,128)(2,1)}, u32[]{:S(2)}) copy-start(bf16[2,128,1408]{2,1,0:T(8,128)(2,1)} %cot_ref.5) | copy-start | bytes 2162692
  8.7 13.4 %copy-start.4 = (s32[2]{0:T(128)S(1)}, s32[2]{0:T(128)}, u32[]{:S(2)}) copy-start(s32[2]{0:T(128)} %exits_ref.3) | copy-start | bytes 28
  8.7 4.7 %collective-permute-start = (f32[128,1408]{1,0:T(8,128)S(1)}, f32[128,1408]{1,0:T(8,128)S(1)}, u32[]{:S(2)}, u32[]{:S(2)}) collective-permute-start(f32[128,1408]{1,0:T(8,128)S(1)} %get-tuple-element.59), channel_id=1, source_target_pairs={{0,16},{16,0},{1,17},{17,1},{2,18},{18,2},{3,19},{19,3},{4,20},{20... | collective-permute-start | bytes 2162696 | tf_op jit(solution)/shard_map/ppermute | solution.py:30
  9.2 7.7 %collective-permute-start.2 = (bf16[704,128]{1,0:T(8,128)(2,1)S(1)}, bf16[704,128]{1,0:T(8,128)(2,1)S(1)}, u32[]{:S(2)}, u32[]{:S(2)}) collective-permute-start(bf16[704,128]{1,0:T(8,128)(2,1)S(1)} %get-tuple-element.61), channel_id=1, source_target_pairs={{0,2},{2,0},{4,6},{6,4},{8,10},{10,8},{12,14},{14,12},{1,3},{3,1},... | collective-permute-start | bytes 540680 | tf_op jit(solution)/shard_map/ppermute | solution.py:392
  11.8 7.4 %collective-permute-start.3 = (bf16[704,128]{1,0:T(8,128)(2,1)S(1)}, bf16[704,128]{1,0:T(8,128)(2,1)S(1)}, u32[]{:S(2)}, u32[]{:S(2)}) collective-permute-start(bf16[704,128]{1,0:T(8,128)(2,1)S(1)} %get-tuple-element.62), channel_id=1, source_target_pairs={{0,4},{2,6},{4,0},{6,2},{8,12},{10,14},{12,8},{14,10},{1,5},{3,7},... | collective-permute-start | bytes 540680 | tf_op jit(solution)/shard_map/ppermute | solution.py:392
  13.4 8.7 %collective-permute-start.4 = (bf16[704,128]{1,0:T(8,128)(2,1)S(1)}, bf16[704,128]{1,0:T(8,128)(2,1)S(1)}, u32[]{:S(2)}, u32[]{:S(2)}) collective-permute-start(bf16[704,128]{1,0:T(8,128)(2,1)S(1)} %get-tuple-element.63), channel_id=1, source_target_pairs={{0,6},{2,4},{4,2},{6,0},{8,14},{10,12},{12,10},{14,8},{1,7},{3,5},... | collective-permute-start | bytes 540680 | tf_op jit(solution)/shard_map/ppermute | solution.py:392
  14.3 7.7 %collective-permute-start.1 = (f32[8,128]{1,0:T(8,128)S(1)}, f32[8,128]{1,0:T(8,128)S(1)}, u32[]{:S(2)}, u32[]{:S(2)}) collective-permute-start(f32[8,128]{1,0:T(8,128)S(1)} %shard_map.96.sums_ref), channel_id=1, source_target_pairs={{0,17},{1,16},{16,1},{17,0},{2,19},{3,18},{18,3},{19,2},{4,21},{5,... | collective-permute-start | bytes 12296 | tf_op jit(solution)/shard_map/ppermute | solution.py:34
  24.1 10.6 %collective-permute-start.5 = (bf16[1408,128]{1,0:T(8,128)(2,1)S(1)}, bf16[1408,128]{1,0:T(8,128)(2,1)S(1)}, u32[]{:S(2)}, u32[]{:S(2)}) collective-permute-start(bf16[1408,128]{1,0:T(8,128)(2,1)S(1)} %get-tuple-element.66), channel_id=1, source_target_pairs={{0,17},{1,16},{16,1},{17,0},{2,19},{3,18},{18,3},{19,2},{4,21},{5,... | collective-permute-start | bytes 1081352 | tf_op jit(solution)/shard_map/ppermute | solution.py:34
  24.8 14.7 %collective-permute-start.11 = (bf16[128,1408]{1,0:T(8,128)(2,1)S(1)}, bf16[128,1408]{1,0:T(8,128)(2,1)S(1)}, u32[]{:S(2)}, u32[]{:S(2)}) collective-permute-start(bf16[128,1408]{1,0:T(8,128)(2,1)S(1)} %get-tuple-element.65.db_ref.refs_4_), channel_id=1, source_target_pairs={{0,6},{2,4},{4,2},{6,0},{8,14},{10,12},{12,10},{14,8},{1,7},{3,5},... | collective-permute-start | bytes 1081352 | tf_op jit(solution)/shard_map/ppermute | solution.py:392
  27.3 17.3 %collective-permute-start.10 = (bf16[128,1408]{1,0:T(8,128)(2,1)S(1)}, bf16[128,1408]{1,0:T(8,128)(2,1)S(1)}, u32[]{:S(2)}, u32[]{:S(2)}) collective-permute-start(bf16[128,1408]{1,0:T(8,128)(2,1)S(1)} %get-tuple-element.65.db_ref.refs_4_), channel_id=1, source_target_pairs={{0,4},{2,6},{4,0},{6,2},{8,12},{10,14},{12,8},{14,10},{1,5},{3,7},... | collective-permute-start | bytes 1081352 | tf_op jit(solution)/shard_map/ppermute | solution.py:392
  27.8 17.0 %collective-permute-start.9 = (bf16[128,1408]{1,0:T(8,128)(2,1)S(1)}, bf16[128,1408]{1,0:T(8,128)(2,1)S(1)}, u32[]{:S(2)}, u32[]{:S(2)}) collective-permute-start(bf16[128,1408]{1,0:T(8,128)(2,1)S(1)} %get-tuple-element.65.db_ref.refs_4_), channel_id=1, source_target_pairs={{0,2},{2,0},{4,6},{6,4},{8,10},{10,8},{12,14},{14,12},{1,3},{3,1},... | collective-permute-start | bytes 1081352 | tf_op jit(solution)/shard_map/ppermute | solution.py:392
  35.7 1.3 %collective-permute-start.7 = (f32[8,1408]{1,0:T(8,128)S(1)}, f32[8,1408]{1,0:T(8,128)S(1)}, u32[]{:S(2)}, u32[]{:S(2)}) collective-permute-start(f32[8,1408]{1,0:T(8,128)S(1)} %get-tuple-element.71), channel_id=1, source_target_pairs={{0,16},{16,0},{1,17},{17,1},{2,18},{18,2},{3,19},{19,3},{4,20},{20... | collective-permute-start | bytes 135176 | tf_op jit(solution)/shard_map/ppermute | solution.py:30
  37.0 8.7 %collective-permute-start.8 = (f32[8,1408]{1,0:T(8,128)S(1)}, f32[8,1408]{1,0:T(8,128)S(1)}, u32[]{:S(2)}, u32[]{:S(2)}) collective-permute-start(f32[8,1408]{1,0:T(8,128)S(1)} %add.6), channel_id=1, source_target_pairs={{0,2},{2,0},{4,6},{6,4},{8,10},{10,8},{12,14},{14,12},{1,3},{3,1},... | collective-permute-start | bytes 135176 | tf_op jit(solution)/shard_map/ppermute | solution.py:392
  38.9 5.8 %collective-permute-start.6 = (f32[8,128]{1,0:T(8,128)S(1)}, f32[8,128]{1,0:T(8,128)S(1)}, u32[]{:S(2)}, u32[]{:S(2)}) collective-permute-start(f32[8,128]{1,0:T(8,128)S(1)} %get-tuple-element.70.inner_ref), channel_id=1, source_target_pairs={{0,17},{1,16},{16,1},{17,0},{2,19},{3,18},{18,3},{19,2},{4,21},{5,... | collective-permute-start | bytes 12296 | tf_op jit(solution)/shard_map/ppermute | solution.py:34
  46.1 18.2 %collective-permute-start.12 = (bf16[4,704,128]{2,1,0:T(8,128)(2,1)S(1)}, bf16[4,704,128]{2,1,0:T(8,128)(2,1)S(1)}, u32[]{:S(2)}, u32[]{:S(2)}) collective-permute-start(bf16[4,704,128]{2,1,0:T(8,128)(2,1)S(1)} %shard_map.100.own_ref), channel_id=1, source_target_pairs={{0,17},{1,16},{16,1},{17,0},{2,19},{3,18},{18,3},{19,2},{4,21},{5,... | collective-permute-start | bytes 2162696 | tf_op jit(solution)/shard_map/ppermute | solution.py:34
  46.5 20.6 %collective-permute-start.15 = (bf16[128,1408]{1,0:T(8,128)(2,1)S(1)}, bf16[128,1408]{1,0:T(8,128)(2,1)S(1)}, u32[]{:S(2)}, u32[]{:S(2)}) collective-permute-start(bf16[128,1408]{1,0:T(8,128)(2,1)S(1)} %get-tuple-element.85.refs_0_), channel_id=1, source_target_pairs={{0,6},{2,4},{4,2},{6,0},{8,14},{10,12},{12,10},{14,8},{1,7},{3,5},... | collective-permute-start | bytes 1081352 | tf_op jit(solution)/shard_map/ppermute | solution.py:392
  49.1 18.0 %collective-permute-start.14 = (bf16[128,1408]{1,0:T(8,128)(2,1)S(1)}, bf16[128,1408]{1,0:T(8,128)(2,1)S(1)}, u32[]{:S(2)}, u32[]{:S(2)}) collective-permute-start(bf16[128,1408]{1,0:T(8,128)(2,1)S(1)} %get-tuple-element.85.refs_0_), channel_id=1, source_target_pairs={{0,4},{2,6},{4,0},{6,2},{8,12},{10,14},{12,8},{14,10},{1,5},{3,7},... | collective-permute-start | bytes 1081352 | tf_op jit(solution)/shard_map/ppermute | solution.py:392
  49.6 17.5 %collective-permute-start.13 = (bf16[128,1408]{1,0:T(8,128)(2,1)S(1)}, bf16[128,1408]{1,0:T(8,128)(2,1)S(1)}, u32[]{:S(2)}, u32[]{:S(2)}) collective-permute-start(bf16[128,1408]{1,0:T(8,128)(2,1)S(1)} %get-tuple-element.85.refs_0_), channel_id=1, source_target_pairs={{0,2},{2,0},{4,6},{6,4},{8,10},{10,8},{12,14},{14,12},{1,3},{3,1},... | collective-permute-start | bytes 1081352 | tf_op jit(solution)/shard_map/ppermute | solution.py:392
  50.0 17.1 %collective-permute-start.16 = (f32[8,1408]{1,0:T(8,128)S(1)}, f32[8,1408]{1,0:T(8,128)S(1)}, u32[]{:S(2)}, u32[]{:S(2)}) collective-permute-start(f32[8,1408]{1,0:T(8,128)S(1)} %add.7.refs_0_), channel_id=1, source_target_pairs={{0,4},{2,6},{4,0},{6,2},{8,12},{10,14},{12,8},{14,10},{1,5},{3,7},... | collective-permute-start | bytes 135176 | tf_op jit(solution)/shard_map/ppermute | solution.py:392
  68.9 3.0 %collective-permute-start.17 = (f32[352,896]{1,0:T(8,128)S(1)}, f32[352,896]{1,0:T(8,128)S(1)}, u32[]{:S(2)}, u32[]{:S(2)}) collective-permute-start(f32[352,896]{1,0:T(8,128)S(1)} %get-tuple-element.94), channel_id=1, source_target_pairs={{0,16},{16,0},{1,17},{17,1},{2,18},{18,2},{3,19},{19,3},{4,20},{20... | collective-permute-start | bytes 3784712 | tf_op jit(solution)/shard_map/ppermute | solution.py:30
  69.9 4.9 %collective-permute-start.18 = (f32[352,512]{1,0:T(8,128)S(1)}, f32[352,512]{1,0:T(8,128)S(1)}, u32[]{:S(2)}, u32[]{:S(2)}) collective-permute-start(f32[352,512]{1,0:T(8,128)S(1)} %get-tuple-element.99), channel_id=1, source_target_pairs={{0,16},{16,0},{1,17},{17,1},{2,18},{18,2},{3,19},{19,3},{4,20},{20... | collective-permute-start | bytes 2162696 | tf_op jit(solution)/shard_map/ppermute | solution.py:30
  72.1 3.6 %collective-permute-start.20 = (f32[128,1408]{1,0:T(8,128)S(1)}, f32[128,1408]{1,0:T(8,128)S(1)}, u32[]{:S(2)}, u32[]{:S(2)}) collective-permute-start(f32[128,1408]{1,0:T(8,128)S(1)} %get-tuple-element.102.total_ref), channel_id=1, source_target_pairs={{0,16},{16,0},{1,17},{17,1},{2,18},{18,2},{3,19},{19,3},{4,20},{20... | collective-permute-start | bytes 2162696 | tf_op jit(solution)/shard_map/ppermute | solution.py:30
  72.3 26.3 %collective-permute-start.21 = (bf16[192,896]{1,0:T(8,128)(2,1)S(1)}, bf16[192,896]{1,0:T(8,128)(2,1)S(1)}, u32[]{:S(2)}, u32[]{:S(2)}) collective-permute-start(bf16[192,896]{1,0:T(8,128)(2,1)S(1)} %get-tuple-element.97), channel_id=1, source_target_pairs={{0,8},{2,10},{4,12},{6,14},{8,0},{10,2},{12,4},{14,6},{1,9},{3,11}... | collective-permute-start | bytes 1032200 | tf_op jit(solution)/shard_map/ppermute | solution.py:392
  75.0 23.7 %collective-permute-start.19 = (bf16[176,512]{1,0:T(8,128)(2,1)S(1)}, bf16[176,512]{1,0:T(8,128)(2,1)S(1)}, u32[]{:S(2)}, u32[]{:S(2)}) collective-permute-start(bf16[176,512]{1,0:T(8,128)(2,1)S(1)} %get-tuple-element.100), channel_id=1, source_target_pairs={{0,8},{2,10},{4,12},{6,14},{8,0},{10,2},{12,4},{14,6},{1,9},{3,11}... | collective-permute-start | bytes 540680 | tf_op jit(solution)/shard_map/ppermute | solution.py:392
where the time goes:
time: 100 us
  waiting for transfers between devices  56.5 us (56%)
  starting transfers between devices  22.4 us (22%)
  Pallas kernels  18.5 us (18%)
  local copies, waits for them, and re-layouts  1.39 us (1%)
    ppermute x13, waiting for transfers between devices, across(): return lax.ppermute(value, 'dp', [(i, i ^ distance) for i in range(chips)])  36.3 us
    pallas_call x15, Pallas kernels, call(): pl.pallas_call(kernel, out_shape=shapes, in_specs=list(specs), out_specs=...  18.5 us
    ppermute x13, starting transfers between devices, across(): return lax.ppermute(value, 'dp', [(i, i ^ distance) for i in range(chips)])  18.1 us
    ppermute x4, waiting for transfers between devices, opposite(): lax.ppermute(value, ('section', 'mp'), [(i, 3 - i) for i in range(4)])  17.9 us
    ppermute x4, starting transfers between devices, opposite(): lax.ppermute(value, ('section', 'mp'), [(i, 3 - i) for i in range(4)])  2.59 us
    ppermute x5, waiting for transfers between devices, swap(): return lax.ppermute(value, axis, [(0, 1), (1, 0)])  2.31 us
  transfers between devices with their start and end apart: 22, of which 12 were waited for; matrix products, arithmetic and copies ran while one was open for 0% of the time, Pallas kernels for 7%

commit v1 on v0

--- a/solution.py
+++ b/solution.py
@@ -55,45 +55,61 @@
     return jnp.concatenate([packed] * 16, axis=0).T
 
 
-def load(stash, weight, chips, group):
-    slots, rows, features = stash.shape
-    block = features // (2 * chips)
-    groups = chips // group
-    height = 2 * groups * block
-    parts = chunks_of(features, 512)
-
-    def kernel(stash_hbm, weight_hbm, w, x, *refs):
-        *out_refs, turned, sems = refs
-        copy = pltpu.make_async_copy(stash_hbm, x, sems.at[len(parts)])
-        copy.start()
+def load(weight):
+    parts = chunks_of(weight.shape[0], 512)
+
+    def kernel(weight_hbm, w, sems):
         copies = []
         for index, (start, size) in enumerate(parts):
             part = pl.ds(start, size)
             copies.append(pltpu.make_async_copy(weight_hbm.at[part], w.at[part], sems.at[index]))
             copies[-1].start()
-        copy.wait()
-        turned[...] = x[own_slot()].T
+        for copy in copies:
+            copy.wait()
+
+    return call(
+        kernel,
+        [(weight.shape, bf16)],
+        [(HBM, weight)],
+        [pltpu.SemaphoreType.DMA((len(parts),))],
+        limit=42,
+    )[0]
+
+
+def forward(stash, weight, injection, order, chips, group):
+    slots, rows, features = stash.shape
+    half = weight.shape[1]
+    block = features // (2 * chips)
+    groups = chips // group
+    height = 2 * groups * block
+
+    def kernel(order_ref, stash_ref, weight_ref, inj_ref, keep_ref, send_ref, *refs):
+        *out_refs, turned, acc = refs
+        slot = own_slot()
+        left = stash_ref[...].reshape(slots * rows, features)
+        for start, size in chunks_of(half, 512):
+            part = slice(start, start + size)
+            term = jnp.dot(left, weight_ref[:, part], preferred_element_type=f32)
+            acc[:, :, part] = term.reshape(slots, rows, size)
+        keep_ref[...] = acc[slot] + inj_ref[order_ref[0, slot]].astype(f32)
+        send_ref[...] = acc[1 - slot] + inj_ref[order_ref[0, 1 - slot]].astype(f32)
+        if out_refs:
+            turned[...] = stash_ref[slot].T
         dp = lax.axis_index("dp")
         for distance, out_ref in enumerate(out_refs):
-            for half in range(2):
+            for half_index in range(2):
                 for other in range(groups):
                     chip = dp ^ (distance + group * other)
-                    source = pl.multiple_of((half * chips + chip) * block, 16)
-                    base = (half * groups + other) * block
+                    source = pl.multiple_of((half_index * chips + chip) * block, 16)
+                    base = (half_index * groups + other) * block
                     out_ref[base : base + block] = turned[pl.ds(source, block)]
-        for each in copies:
-            each.wait()
 
     pieces = group if block % 16 == 0 else 0
-    weight, loaded, *columns = call(
-        kernel,
-        [(weight.shape, bf16), (stash.shape, bf16)] + [((height, rows), bf16)] * pieces,
-        [(HBM, stash), (HBM, weight)],
-        [
-            pltpu.VMEM((features, rows), bf16),
-            pltpu.SemaphoreType.DMA((len(parts) + 1,)),
-        ],
-        limit=42,
+    keep, send, *columns = call(
+        kernel,
+        [((rows, half), f32)] * 2 + [((height, rows), bf16)] * pieces,
+        [(SMEM, order), (VMEM, stash), (VMEM, weight), (VMEM, injection)],
+        [pltpu.VMEM((features, rows), bf16), pltpu.VMEM((slots, rows, half), f32)],
     )
     if not columns:
         turned = lax.dynamic_index_in_dim(stash, own_slot(), 0, keepdims=False).T
@@ -106,29 +122,7 @@
                 for other in range(groups)
             ]
             columns.append(jnp.stack(picked, axis=1).reshape(height, rows))
-    return weight, loaded, columns
-
-
-def forward(stash, weight, injection, order):
-    slots, rows, features = stash.shape
-    half = weight.shape[1]
-
-    def kernel(order_ref, stash_ref, weight_ref, inj_ref, keep_ref, send_ref, acc):
-        slot = own_slot()
-        left = stash_ref[...].reshape(slots * rows, features)
-        for start, size in chunks_of(half, 512):
-            part = slice(start, start + size)
-            term = jnp.dot(left, weight_ref[:, part], preferred_element_type=f32)
-            acc[:, :, part] = term.reshape(slots, rows, size)
-        keep_ref[...] = acc[slot] + inj_ref[order_ref[0, slot]].astype(f32)
-        send_ref[...] = acc[1 - slot] + inj_ref[order_ref[0, 1 - slot]].astype(f32)
-
-    return call(
-        kernel,
-        [((rows, half), f32)] * 2,
-        [(SMEM, order), (VMEM, stash), (VMEM, weight), (VMEM, injection)],
-        [pltpu.VMEM((slots, rows, half), f32)],
-    )
+    return keep, send, columns
 
 
 def row_sums(order, cotangent, gain, keep, got):
@@ -302,39 +296,21 @@
     )
 
 
-def chip_sum(keep, other, block, gains=()):
+def chip_sum(keep, other, block):
     height, width = keep.shape
-    extra = 16 if gains else 0
-
-    def kernel(keep_ref, other_ref, *refs):
-        gain_refs, (own_ref, *away_refs) = refs[: len(gains)], refs[len(gains) :]
+
+    def kernel(keep_ref, other_ref, own_ref, *away_refs):
         total = keep_ref[...] + other_ref[...]
         own_ref[...] = total[:block]
         for index, away_ref in enumerate(away_refs):
-            away_ref[:block] = total[(index + 1) * block : (index + 2) * block].astype(bf16)
-        if gains:
-            rest = group_gains(gain_refs)
-            half = rest.shape[1]
-            packed = []
-            for _ in range(3):
-                high = rest.astype(bf16).astype(f32)
-                rest = rest - high
-                tail = high[:, half - width :]
-                packed += [high[:, :width], tail]
-            packed.append(jnp.zeros((extra - len(packed), width), f32))
-            for away_ref in away_refs:
-                away_ref[block:] = jnp.concatenate(packed, axis=0).astype(bf16)
-
-    outs = [((block, width), f32)] + [((block + extra, width), bf16)] * (height // block - 1)
-    return call(kernel, outs, [(VMEM, value) for value in (keep, other, *gains)])
-
-
-def group_gains(refs):
-    return refs[0][:1] + refs[1][:1]
+            away_ref[...] = total[(index + 1) * block : (index + 2) * block].astype(bf16)
+
+    outs = [((block, width), f32)] + [((block, width), bf16)] * (height // block - 1)
+    return call(kernel, outs, [(VMEM, keep), (VMEM, other)])
 
 
 def final_sum(own, others, gains, half):
-    block, first_width = own[0].shape
+    block = own[0].shape[0]
     count = len(others[0])
 
     def kernel(*refs):
@@ -345,24 +321,18 @@
             own_ref, *other_refs = refs[part * (count + 1) : (part + 1) * (count + 1)]
             total = own_ref[...]
             for other_ref in other_refs:
-                total = total + other_ref[:block].astype(f32)
+                total = total + other_ref[...].astype(f32)
             width = own_ref.shape[1]
             weight_out[:, start : start + width] = total
             start += width
-        sums = [group_gains(gain_refs)]
-        for ref in refs[1 : count + 1]:
-            packed = ref[block:].astype(f32)
-            heads = packed[0:1] + packed[2:3] + packed[4:5]
-            tails = packed[1:2] + packed[3:4] + packed[5:6]
-            tails = tails[:, 2 * first_width - half :]
-            sums.append(jnp.concatenate([heads, tails], axis=1))
+        sums = [ref[:1] for ref in gain_refs]
         while len(sums) > 1:
             sums = [a + b for a, b in zip(sums[::2], sums[1::2])]
-        gain_out[...] = sums[0]
+        gain_out[...] = sums[0].reshape(half)
 
     values = [value for mine, theirs in zip(own, others) for value in (mine, *theirs)]
     ins = [(VMEM, value) for value in (*gains, *values)]
-    return call(kernel, [((block, half), f32), ((1, half), f32)], ins)
+    return call(kernel, [((block, half), f32), ((half,), f32)], ins)
 
 
 def place(order, total, other):
@@ -395,11 +365,10 @@
         return [value] + [across(value, distance) for distance in range(1, group)]
 
     block = features // (2 * chips)
-    weight, stash, columns = load(stash, weight, chips, group)
+    gain = gain.reshape(1, half)
+    weight = load(weight)
+    keep, send, columns = forward(stash, weight, injection, order, chips, group)
     columns = columns[:1] + [across(columns[distance], distance) for distance in range(1, group)]
-
-    gain = gain.reshape(1, half)
-    keep, send = forward(stash, weight, injection, order)
     got = swap(send, "section")
     sums = row_sums(order, cotangent, gain, keep, got)
     others = opposite(sums)
@@ -430,10 +399,11 @@
     left = left_side(columns, opposite(columns))
 
     gains = gains + near_gains
-    gains = [gains, across(gains, 2)]
-    left, grads0, gains = lax.optimization_barrier((left, grads0, gains))
-
-    cut = (half * 9 // 16 + 127) // 128 * 128
+    far_gains = across(gains, 2)
+    left, grads0, far_gains = lax.optimization_barrier((left, grads0, far_gains))
+    gains = gains + far_gains
+
+    cut = (half // 2 + 127) // 128 * 128
     terms = [
         weight_terms(left, grads0 + grads1, lanes) for lanes in [(0, cut), (cut, half - cut)]
     ]
@@ -443,13 +413,15 @@
         if part:
             keep, *_ = lax.optimization_barrier((keep, *aways))
             total, *_ = lax.optimization_barrier((total, *aways))
-        mine, *aways = chip_sum(keep, arrived[part], block, () if part else gains)
+        mine, *aways = chip_sum(keep, arrived[part], block)
         own.append(mine)
         others.append([across(away, group * (i + 1)) for i, away in enumerate(aways)])
+    gains, *_ = lax.optimization_barrier((gains, *aways))
+    gains = [gains] + [across(gains, group * other) for other in range(1, groups)]
     d_injection = place(order, total, swap(total, "section"))
     others[1], d_injection = lax.optimization_barrier((others[1], d_injection))
     d_weight, d_gain = final_sum(own, others, gains, half)
-    return (d_injection, d_weight, d_gain[0])
+    return (d_injection, d_weight, d_gain)
 
 
 def solution(mesh):

time: 100 us -> 98.9 us (0.989)
  starting transfers between devices: 22.4 us -> 24.6 us
  waiting for transfers between devices: 56.5 us -> 54.3 us
    ppermute x13 -> x14, starting transfers between devices: 18.1 us -> 20.3 us  [across(): return lax.ppermute(value, 'dp', [(i, i ^ distance) for i in range(chips)])]
    ppermute x13 -> x14, waiting for transfers between devices: 36.3 us -> 34.7 us  [across(): return lax.ppermute(value, 'dp', [(i, i ^ distance) for i in range(chips)])]
  transfers between devices with their start and end apart: 22 -> 23, of which waited for: 12 -> 13; matrix products, arithmetic and copies ran while one was open for 0% -> 0% of each run, Pallas kernels for 7% -> 7%
where the time goes in v1:
time: 98.9 us; the launch traced here: 98.7 us
  waiting for transfers between devices  54.3 us (55%)
  starting transfers between devices  24.6 us (25%)
  Pallas kernels  18.5 us (19%)
    ppermute x14, waiting for transfers between devices, across(): return lax.ppermute(value, 'dp', [(i, i ^ distance) for i in range(chips)])  34.7 us
    ppermute x14, starting transfers between devices, across(): return lax.ppermute(value, 'dp', [(i, i ^ distance) for i in range(chips)])  20.3 us
    pallas_call x15, Pallas kernels, call(): pl.pallas_call(kernel, out_shape=shapes, in_specs=list(specs), out_specs=...  18.5 us
    ppermute x4, waiting for transfers between devices, opposite(): lax.ppermute(value, ('section', 'mp'), [(i, 3 - i) for i in range(4)])  18 us
    ppermute x4, starting transfers between devices, opposite(): lax.ppermute(value, ('section', 'mp'), [(i, 3 - i) for i in range(4)])  2.57 us
  transfers between devices with their start and end apart: 23, of which 13 were waited for; matrix products, arithmetic and copies ran while one was open for 0% of the time, Pallas kernels for 7%

profile of v1, /device:TPU:0, one launch (start us, length us, event | category | flops | bytes accessed | tf_op | source)
XLA Modules:
  0.0 98.7 jit_solution(18246012781374301204)
XLA Ops:
  0.6 0.0 copy-start.3
  0.6 0.0 copy-start.2
  0.7 3.4 %shard_map.94.weight_ref = bf16[2816,1408]{1,0:T(8,128)(2,1)S(1)} custom-call(bf16[2816,1408]{1,0:T(8,128)(2,1)} %weight_hbm.1), custom_call_target="tpu_custom_call" | custom-call | flops 1000 | bytes 1000 | tf_op jit(solution)/shard_map/pallas_call | solution.py:18
  4.1 0.4 copy-done.1
  4.6 3.1 %shard_map.95 = (f32[128,1408]{1,0:T(8,128)S(1)}, f32[128,1408]{1,0:T(8,128)S(1)}, bf16[704,128]{1,0:T(8,128)(2,1)S(1)}, bf16[704,128]{1,0:T(8,128)(2,1)S(1)}, b...) custom-call(s32[1,2]{1,0:T(1,128)S(1)} %copy-done.3, bf16[2,128,2816]{2,1,0:T(8,128)(2,1)S(1)} %bitcast.1, ...), custom_call_target="tpu_custom_call" | custom-call | flops 1000 | bytes 1000 | tf_op jit(solution)/shard_map/pallas_call | solution.py:18
  7.7 0.0 copy-start.4
  7.7 0.5 collective-permute-start
  8.2 2.6 %collective-permute-start.2 = (bf16[704,128]{1,0:T(8,128)(2,1)S(1)}, bf16[704,128]{1,0:T(8,128)(2,1)S(1)}, u32[]{:S(2)}, u32[]{:S(2)}) collective-permute-start(bf16[704,128]{1,0:T(8,128)(2,1)S(1)} %get-tuple-element.57), channel_id=1, source_target_pairs={{0,2},{2,0},{4,6},{6,4},{8,10},{10,8},{12,14},{14,12},{1,3},{3,1},... | collective-permute-start | bytes 540680 | tf_op jit(solution)/shard_map/ppermute | solution.py:362
  10.8 1.6 %collective-permute-start.3 = (bf16[704,128]{1,0:T(8,128)(2,1)S(1)}, bf16[704,128]{1,0:T(8,128)(2,1)S(1)}, u32[]{:S(2)}, u32[]{:S(2)}) collective-permute-start(bf16[704,128]{1,0:T(8,128)(2,1)S(1)} %get-tuple-element.58), channel_id=1, source_target_pairs={{0,4},{2,6},{4,0},{6,2},{8,12},{10,14},{12,8},{14,10},{1,5},{3,7},... | collective-permute-start | bytes 540680 | tf_op jit(solution)/shard_map/ppermute | solution.py:362
  12.4 0.0 collective-permute-start.4
  12.4 0.0 collective-permute-done.got_ref
  12.4 0.9 shard_map.96.sums_ref
  13.3 1.1 %collective-permute-start.1 = (f32[8,128]{1,0:T(8,128)S(1)}, f32[8,128]{1,0:T(8,128)S(1)}, u32[]{:S(2)}, u32[]{:S(2)}) collective-permute-start(f32[8,128]{1,0:T(8,128)S(1)} %shard_map.96.sums_ref), channel_id=1, source_target_pairs={{0,17},{1,16},{16,1},{17,0},{2,19},{3,18},{18,3},{19,2},{4,21},{5,... | collective-permute-start | bytes 12296 | tf_op jit(solution)/shard_map/ppermute | solution.py:34
  14.4 1.5 %collective-permute-done.2.refs_1_ = bf16[704,128]{1,0:T(8,128)(2,1)S(1)} collective-permute-done((bf16[704,128]{1,0:T(8,128)(2,1)S(1)}, bf16[704,128]{1,0:T(8,128)(2,1)S(1)}, u32[]{:S(2)}, u32[]{:S(2)}) %collective-permute-start.2) | collective-permute-done | bytes 180256 | tf_op jit(solution)/shard_map/ppermute | solution.py:362
  15.9 2.3 %collective-permute-done.3.refs_2_ = bf16[704,128]{1,0:T(8,128)(2,1)S(1)} collective-permute-done((bf16[704,128]{1,0:T(8,128)(2,1)S(1)}, bf16[704,128]{1,0:T(8,128)(2,1)S(1)}, u32[]{:S(2)}, u32[]{:S(2)}) %collective-permute-start.3) | collective-permute-done | bytes 180256 | tf_op jit(solution)/shard_map/ppermute | solution.py:362
  18.2 2.9 %collective-permute-done.4.refs_3_ = bf16[704,128]{1,0:T(8,128)(2,1)S(1)} collective-permute-done((bf16[704,128]{1,0:T(8,128)(2,1)S(1)}, bf16[704,128]{1,0:T(8,128)(2,1)S(1)}, u32[]{:S(2)}, u32[]{:S(2)}) %collective-permute-start.4) | collective-permute-done | bytes 180256 | tf_op jit(solution)/shard_map/ppermute | solution.py:362
  21.1 0.0 collective-permute-done.1.others_ref
  21.1 2.1 %shard_map.97 = (bf16[128,1408]{1,0:T(8,128)(2,1)S(1)}, f32[128,1408]{1,0:T(8,128)S(1)}, f32[1,1408]{1,0:T(1,128)S(1)}, bf16[1408,128]{1,0:T(8,128)(2,1)S(1)}) custom-call(s32[1,2]{1,0:T(1,128)S(1)} %copy-done.3, s32[2]{0:T(128)S(1)} %copy-done.4, bf16[2,128,1408]{2,1,0:T(8,128)(2,1)S(1)} %copy-done, f32[1,1408]{1,0:T(1,128)S(1)} %reshape.9.gain_ref, ...), custom_call_target="tpu_custom_call" | custom-call | flops 1000 | bytes 1000 | tf_op jit(solution)/shard_map/pallas_call | solution.py:18
  23.1 0.7 collective-permute-start.5
  23.8 2.5 %collective-permute-start.11 = (bf16[128,1408]{1,0:T(8,128)(2,1)S(1)}, bf16[128,1408]{1,0:T(8,128)(2,1)S(1)}, u32[]{:S(2)}, u32[]{:S(2)}) collective-permute-start(bf16[128,1408]{1,0:T(8,128)(2,1)S(1)} %get-tuple-element.61.db_ref.refs_4_), channel_id=1, source_target_pairs={{0,6},{2,4},{4,2},{6,0},{8,14},{10,12},{12,10},{14,8},{1,7},{3,5},... | collective-permute-start | bytes 1081352 | tf_op jit(solution)/shard_map/ppermute | solution.py:362
  26.3 0.5 collective-permute-start.10
  26.8 0.5 collective-permute-start.9
  27.3 1.2 %shard_map.98.kept_ref = f32[1408,128]{1,0:T(8,128)S(1)} custom-call(bf16[128,1408]{1,0:T(8,128)(2,1)S(1)} %get-tuple-element.61.db_ref.refs_4_, bf16[2816,1408]{1,0:T(8,128)(2,1)S(1)} %shard_map.94.weight_ref), custom_call_target="tpu_custom_call" | custom-call | flops 1000 | bytes 1000 | tf_op jit(solution)/shard_map/pallas_call | solution.py:18
  28.5 5.2 %collective-permute-done.5.sent_ref = bf16[1408,128]{1,0:T(8,128)(2,1)S(1)} collective-permute-done((bf16[1408,128]{1,0:T(8,128)(2,1)S(1)}, bf16[1408,128]{1,0:T(8,128)(2,1)S(1)}, u32[]{:S(2)}, u32[]{:S(2)}) %collective-permute-start.5) | collective-permute-done | bytes 360480 | tf_op jit(solution)/shard_map/ppermute | solution.py:34
  33.7 1.0 %shard_map.99 = (f32[128,1408]{1,0:T(8,128)S(1)}, f32[8,128]{1,0:T(8,128)S(1)}, f32[8,1408]{1,0:T(8,128)S(1)}) custom-call(s32[1,2]{1,0:T(1,128)S(1)} %copy-done.3, s32[2]{0:T(128)S(1)} %copy-done.4, bf16[2,128,1408]{2,1,0:T(8,128)(2,1)S(1)} %copy-done, f32[1,1408]{1,0:T(1,128)S(1)} %reshape.9.gain_ref, f32[128,1408]{1,0:T(8,128)S(1)} %get-tuple-element.54.keep_ref, ...), custom_call_target="tpu_custom_call" | custom-call | flops 1000 | bytes 1000 | tf_op jit(solution)/shard_map/pallas_call | solution.py:18
  34.7 0.4 collective-permute-start.7
  35.1 0.9 collective-permute-done.7
  36.0 1.9 %collective-permute-start.8 = (f32[8,1408]{1,0:T(8,128)S(1)}, f32[8,1408]{1,0:T(8,128)S(1)}, u32[]{:S(2)}, u32[]{:S(2)}) collective-permute-start(f32[8,1408]{1,0:T(8,128)S(1)} %add.9), channel_id=1, source_target_pairs={{0,2},{2,0},{4,6},{6,4},{8,10},{10,8},{12,14},{14,12},{1,3},{3,1},... | collective-permute-start | bytes 135176 | tf_op jit(solution)/shard_map/ppermute | solution.py:362
  37.9 0.5 collective-permute-start.6
  38.5 0.0 collective-permute-done.11.refs_7_
  38.5 5.1 %collective-permute-done.10.refs_6_ = bf16[128,1408]{1,0:T(8,128)(2,1)S(1)} collective-permute-done((bf16[128,1408]{1,0:T(8,128)(2,1)S(1)}, bf16[128,1408]{1,0:T(8,128)(2,1)S(1)}, u32[]{:S(2)}, u32[]{:S(2)}) %collective-permute-start.10) | collective-permute-done | bytes 360480 | tf_op jit(solution)/shard_map/ppermute | solution.py:362
  43.6 0.1 collective-permute-done.9.refs_5_
  43.7 0.0 collective-permute-done.6.other_ref
  43.7 0.9 collective-permute-done.8
  44.7 0.4 shard_map.101
  45.1 0.3 collective-permute-start.12
  45.5 2.6 %collective-permute-start.15 = (bf16[128,1408]{1,0:T(8,128)(2,1)S(1)}, bf16[128,1408]{1,0:T(8,128)(2,1)S(1)}, u32[]{:S(2)}, u32[]{:S(2)}) collective-permute-start(bf16[128,1408]{1,0:T(8,128)(2,1)S(1)} %get-tuple-element.81.refs_0_), channel_id=1, source_target_pairs={{0,6},{2,4},{4,2},{6,0},{8,14},{10,12},{12,10},{14,8},{1,7},{3,5},... | collective-permute-start | bytes 1081352 | tf_op jit(solution)/shard_map/ppermute | solution.py:362
  48.1 0.5 collective-permute-start.14
  48.6 0.4 collective-permute-start.13
  49.0 1.7 %collective-permute-start.16 = (f32[8,1408]{1,0:T(8,128)S(1)}, f32[8,1408]{1,0:T(8,128)S(1)}, u32[]{:S(2)}, u32[]{:S(2)}) collective-permute-start(f32[8,1408]{1,0:T(8,128)S(1)} %add.10), channel_id=1, source_target_pairs={{0,4},{2,6},{4,0},{6,2},{8,12},{10,14},{12,8},{14,10},{1,5},{3,7},... | collective-permute-start | bytes 135176 | tf_op jit(solution)/shard_map/ppermute | solution.py:362
  50.6 12.7 %collective-permute-done.12.other_ref = bf16[4,704,128]{2,1,0:T(8,128)(2,1)S(1)} collective-permute-done((bf16[4,704,128]{2,1,0:T(8,128)(2,1)S(1)}, bf16[4,704,128]{2,1,0:T(8,128)(2,1)S(1)}, u32[]{:S(2)}, u32[]{:S(2)}) %collective-permute-start.12) | collective-permute-done | bytes 720928 | tf_op jit(solution)/shard_map/ppermute | solution.py:34
  63.4 0.4 shard_map.102.left_ref
  63.8 2.3 %collective-permute-done.16 = f32[8,1408]{1,0:T(8,128)S(1)} collective-permute-done((f32[8,1408]{1,0:T(8,128)S(1)}, f32[8,1408]{1,0:T(8,128)S(1)}, u32[]{:S(2)}, u32[]{:S(2)}) %collective-permute-start.16) | collective-permute-done | bytes 45088 | tf_op jit(solution)/shard_map/ppermute | solution.py:362
  66.1 0.0 collective-permute-done.15.refs_3_
  66.1 0.0 collective-permute-done.14.refs_2_
  66.1 0.0 collective-permute-done.13.refs_1_
  66.1 1.4 %shard_map.104 = (f32[352,768]{1,0:T(8,128)S(1)}, f32[352,768]{1,0:T(8,128)S(1)}) custom-call(bf16[704,1024]{1,0:T(8,128)(2,1)S(1)} %shard_map.102.left_ref, bf16[128,1408]{1,0:T(8,128)(2,1)S(1)} %get-tuple-element.81.refs_0_, bf16[128,1408]{1,0:T(8,128)(2,1)S(1)} %collective-permute-done.13.refs_1_, bf16[128,1408]{1,0:T(8,128)(2,1)S(1)} %collective-permute-done.14.refs_2_, ...), custom_call_target="tpu_custom_call" | custom-call | flops 1000 | bytes 1000 | tf_op jit(solution)/shard_map/pallas_call | solution.py:18
  67.5 0.1 collective-permute-start.17
  67.6 1.4 %shard_map.103 = (f32[352,640]{1,0:T(8,128)S(1)}, f32[352,640]{1,0:T(8,128)S(1)}) custom-call(bf16[704,1024]{1,0:T(8,128)(2,1)S(1)} %shard_map.102.left_ref, bf16[128,1408]{1,0:T(8,128)(2,1)S(1)} %get-tuple-element.81.refs_0_, bf16[128,1408]{1,0:T(8,128)(2,1)S(1)} %collective-permute-done.13.refs_1_, bf16[128,1408]{1,0:T(8,128)(2,1)S(1)} %collective-permute-done.14.refs_2_, ...), custom_call_target="tpu_custom_call" | custom-call | flops 1000 | bytes 1000 | tf_op jit(solution)/shard_map/pallas_call | solution.py:18
  69.0 0.6 collective-permute-start.18
  69.5 0.7 collective-permute-done.17.other_ref
  70.3 0.2 shard_map.105
  70.4 0.2 collective-permute-start.20
  70.6 2.6 %collective-permute-start.22 = (bf16[176,768]{1,0:T(8,128)(2,1)S(1)}, bf16[176,768]{1,0:T(8,128)(2,1)S(1)}, u32[]{:S(2)}, u32[]{:S(2)}) collective-permute-start(bf16[176,768]{1,0:T(8,128)(2,1)S(1)} %get-tuple-element.91), channel_id=1, source_target_pairs={{0,8},{2,10},{4,12},{6,14},{8,0},{10,2},{12,4},{14,6},{1,9},{3,11}... | collective-permute-start | bytes 811016 | tf_op jit(solution)/shard_map/ppermute | solution.py:362
  73.2 0.0 collective-permute-done.18.other_ref
  73.2 0.1 shard_map.106
  73.4 1.0 %collective-permute-start.19 = (bf16[176,640]{1,0:T(8,128)(2,1)S(1)}, bf16[176,640]{1,0:T(8,128)(2,1)S(1)}, u32[]{:S(2)}, u32[]{:S(2)}) collective-permute-start(bf16[176,640]{1,0:T(8,128)(2,1)S(1)} %get-tuple-element.94), channel_id=1, source_target_pairs={{0,8},{2,10},{4,12},{6,14},{8,0},{10,2},{12,4},{14,6},{1,9},{3,11}... | collective-permute-start | bytes 675848 | tf_op jit(solution)/shard_map/ppermute | solution.py:362
  74.4 2.0 %collective-permute-start.21 = (f32[8,1408]{1,0:T(8,128)S(1)}, f32[8,1408]{1,0:T(8,128)S(1)}, u32[]{:S(2)}, u32[]{:S(2)}) collective-permute-start(f32[8,1408]{1,0:T(8,128)S(1)} %add.11.refs_0_), channel_id=1, source_target_pairs={{0,8},{2,10},{4,12},{6,14},{8,0},{10,2},{12,4},{14,6},{1,9},{3,11}... | collective-permute-start | bytes 135176 | tf_op jit(solution)/shard_map/ppermute | solution.py:362
  76.3 0.0 collective-permute-done.20.other_ref
  76.4 1.7 %shard_map.107 = f32[2,128,1408]{2,1,0:T(8,128)} custom-call(s32[1,2]{1,0:T(1,128)S(1)} %copy-done.3, f32[128,1408]{1,0:T(8,128)S(1)} %get-tuple-element.96.total_ref, f32[128,1408]{1,0:T(8,128)S(1)} %collective-permute-done.20.other_ref), custom_call_target="tpu_custom_call" | custom-call | flops 1000 | bytes 1000 | tf_op jit(solution)/shard_map/pallas_call | solution.py:18
  78.1 19.1 %collective-permute-done.19.refs_5_ = bf16[176,640]{1,0:T(8,128)(2,1)S(1)} collective-permute-done((bf16[176,640]{1,0:T(8,128)(2,1)S(1)}, bf16[176,640]{1,0:T(8,128)(2,1)S(1)}, u32[]{:S(2)}, u32[]{:S(2)}) %collective-permute-start.19) | collective-permute-done | bytes 225312 | tf_op jit(solution)/shard_map/ppermute | solution.py:362
  97.2 0.5 collective-permute-done.21.refs_1_
  97.7 0.0 collective-permute-done.22.refs_3_
  97.7 1.1 %shard_map.108 = (f32[176,1408]{1,0:T(8,128)}, f32[1408]{0:T(1024)}) custom-call(f32[8,1408]{1,0:T(8,128)S(1)} %add.11.refs_0_, f32[8,1408]{1,0:T(8,128)S(1)} %collective-permute-done.21.refs_1_, f32[176,768]{1,0:T(8,128)S(1)} %get-tuple-element.100.refs_2_, bf16[176,768]{1,0:T(8,128)(2,1)S(1)} %collective-permute-done.22.refs_3_, ...), custom_call_target="tpu_custom_call" | custom-call | flops 1000 | bytes 1000 | tf_op jit(solution)/shard_map/pallas_call | solution.py:18
  (13 shorter events, 0.1 us)
Async XLA Ops:
  0.6 3.5 %copy-start.3 = (s32[1,2]{1,0:T(1,128)S(1)}, s32[1,2]{1,0:T(1,128)}, u32[]{:S(2)}) copy-start(s32[1,2]{1,0:T(1,128)} %order_ref.9) | copy-start | bytes 28
  0.6 3.5 %copy-start.2 = (bf16[2,128,1408]{2,1,0:T(8,128)(2,1)S(1)}, bf16[2,128,1408]{2,1,0:T(8,128)(2,1)}, u32[]{:S(2)}) copy-start(bf16[2,128,1408]{2,1,0:T(8,128)(2,1)} %inj_ref.1) | copy-start | bytes 2162692
  0.7 3.9 %copy-start.1 = (bf16[1,2,128,2816]{3,2,1,0:T(8,128)(2,1)S(1)}, bf16[1,2,128,2816]{3,2,1,0:T(8,128)(2,1)}, u32[]{:S(2)}) copy-start(bf16[1,2,128,2816]{3,2,1,0:T(8,128)(2,1)} %param.7) | copy-start | bytes 4325380
  4.6 7.8 %copy-start.5 = (f32[1408]{0:T(1024)S(1)}, f32[1408]{0:T(1024)}, u32[]{:S(2)}) copy-start(f32[1408]{0:T(1024)} %param.10) | copy-start | bytes 16900
  4.6 7.8 %copy-start = (bf16[2,128,1408]{2,1,0:T(8,128)(2,1)S(1)}, bf16[2,128,1408]{2,1,0:T(8,128)(2,1)}, u32[]{:S(2)}) copy-start(bf16[2,128,1408]{2,1,0:T(8,128)(2,1)} %cot_ref.5) | copy-start | bytes 2162692
  7.7 13.4 %copy-start.4 = (s32[2]{0:T(128)S(1)}, s32[2]{0:T(128)}, u32[]{:S(2)}) copy-start(s32[2]{0:T(128)} %exits_ref.3) | copy-start | bytes 28
  7.7 4.7 %collective-permute-start = (f32[128,1408]{1,0:T(8,128)S(1)}, f32[128,1408]{1,0:T(8,128)S(1)}, u32[]{:S(2)}, u32[]{:S(2)}) collective-permute-start(f32[128,1408]{1,0:T(8,128)S(1)} %get-tuple-element.55), channel_id=1, source_target_pairs={{0,16},{16,0},{1,17},{17,1},{2,18},{18,2},{3,19},{19,3},{4,20},{20... | collective-permute-start | bytes 2162696 | tf_op jit(solution)/shard_map/ppermute | solution.py:30
  8.2 7.7 %collective-permute-start.2 = (bf16[704,128]{1,0:T(8,128)(2,1)S(1)}, bf16[704,128]{1,0:T(8,128)(2,1)S(1)}, u32[]{:S(2)}, u32[]{:S(2)}) collective-permute-start(bf16[704,128]{1,0:T(8,128)(2,1)S(1)} %get-tuple-element.57), channel_id=1, source_target_pairs={{0,2},{2,0},{4,6},{6,4},{8,10},{10,8},{12,14},{14,12},{1,3},{3,1},... | collective-permute-start | bytes 540680 | tf_op jit(solution)/shard_map/ppermute | solution.py:362
  10.8 7.4 %collective-permute-start.3 = (bf16[704,128]{1,0:T(8,128)(2,1)S(1)}, bf16[704,128]{1,0:T(8,128)(2,1)S(1)}, u32[]{:S(2)}, u32[]{:S(2)}) collective-permute-start(bf16[704,128]{1,0:T(8,128)(2,1)S(1)} %get-tuple-element.58), channel_id=1, source_target_pairs={{0,4},{2,6},{4,0},{6,2},{8,12},{10,14},{12,8},{14,10},{1,5},{3,7},... | collective-permute-start | bytes 540680 | tf_op jit(solution)/shard_map/ppermute | solution.py:362
  12.4 8.7 %collective-permute-start.4 = (bf16[704,128]{1,0:T(8,128)(2,1)S(1)}, bf16[704,128]{1,0:T(8,128)(2,1)S(1)}, u32[]{:S(2)}, u32[]{:S(2)}) collective-permute-start(bf16[704,128]{1,0:T(8,128)(2,1)S(1)} %get-tuple-element.59), channel_id=1, source_target_pairs={{0,6},{2,4},{4,2},{6,0},{8,14},{10,12},{12,10},{14,8},{1,7},{3,5},... | collective-permute-start | bytes 540680 | tf_op jit(solution)/shard_map/ppermute | solution.py:362
  13.3 7.7 %collective-permute-start.1 = (f32[8,128]{1,0:T(8,128)S(1)}, f32[8,128]{1,0:T(8,128)S(1)}, u32[]{:S(2)}, u32[]{:S(2)}) collective-permute-start(f32[8,128]{1,0:T(8,128)S(1)} %shard_map.96.sums_ref), channel_id=1, source_target_pairs={{0,17},{1,16},{16,1},{17,0},{2,19},{3,18},{18,3},{19,2},{4,21},{5,... | collective-permute-start | bytes 12296 | tf_op jit(solution)/shard_map/ppermute | solution.py:34
  23.1 10.6 %collective-permute-start.5 = (bf16[1408,128]{1,0:T(8,128)(2,1)S(1)}, bf16[1408,128]{1,0:T(8,128)(2,1)S(1)}, u32[]{:S(2)}, u32[]{:S(2)}) collective-permute-start(bf16[1408,128]{1,0:T(8,128)(2,1)S(1)} %get-tuple-element.62), channel_id=1, source_target_pairs={{0,17},{1,16},{16,1},{17,0},{2,19},{3,18},{18,3},{19,2},{4,21},{5,... | collective-permute-start | bytes 1081352 | tf_op jit(solution)/shard_map/ppermute | solution.py:34
  23.8 14.7 %collective-permute-start.11 = (bf16[128,1408]{1,0:T(8,128)(2,1)S(1)}, bf16[128,1408]{1,0:T(8,128)(2,1)S(1)}, u32[]{:S(2)}, u32[]{:S(2)}) collective-permute-start(bf16[128,1408]{1,0:T(8,128)(2,1)S(1)} %get-tuple-element.61.db_ref.refs_4_), channel_id=1, source_target_pairs={{0,6},{2,4},{4,2},{6,0},{8,14},{10,12},{12,10},{14,8},{1,7},{3,5},... | collective-permute-start | bytes 1081352 | tf_op jit(solution)/shard_map/ppermute | solution.py:362
  26.3 17.3 %collective-permute-start.10 = (bf16[128,1408]{1,0:T(8,128)(2,1)S(1)}, bf16[128,1408]{1,0:T(8,128)(2,1)S(1)}, u32[]{:S(2)}, u32[]{:S(2)}) collective-permute-start(bf16[128,1408]{1,0:T(8,128)(2,1)S(1)} %get-tuple-element.61.db_ref.refs_4_), channel_id=1, source_target_pairs={{0,4},{2,6},{4,0},{6,2},{8,12},{10,14},{12,8},{14,10},{1,5},{3,7},... | collective-permute-start | bytes 1081352 | tf_op jit(solution)/shard_map/ppermute | solution.py:362
  26.8 16.9 %collective-permute-start.9 = (bf16[128,1408]{1,0:T(8,128)(2,1)S(1)}, bf16[128,1408]{1,0:T(8,128)(2,1)S(1)}, u32[]{:S(2)}, u32[]{:S(2)}) collective-permute-start(bf16[128,1408]{1,0:T(8,128)(2,1)S(1)} %get-tuple-element.61.db_ref.refs_4_), channel_id=1, source_target_pairs={{0,2},{2,0},{4,6},{6,4},{8,10},{10,8},{12,14},{14,12},{1,3},{3,1},... | collective-permute-start | bytes 1081352 | tf_op jit(solution)/shard_map/ppermute | solution.py:362
  34.7 1.3 %collective-permute-start.7 = (f32[8,1408]{1,0:T(8,128)S(1)}, f32[8,1408]{1,0:T(8,128)S(1)}, u32[]{:S(2)}, u32[]{:S(2)}) collective-permute-start(f32[8,1408]{1,0:T(8,128)S(1)} %get-tuple-element.67), channel_id=1, source_target_pairs={{0,16},{16,0},{1,17},{17,1},{2,18},{18,2},{3,19},{19,3},{4,20},{20... | collective-permute-start | bytes 135176 | tf_op jit(solution)/shard_map/ppermute | solution.py:30
  36.0 8.7 %collective-permute-start.8 = (f32[8,1408]{1,0:T(8,128)S(1)}, f32[8,1408]{1,0:T(8,128)S(1)}, u32[]{:S(2)}, u32[]{:S(2)}) collective-permute-start(f32[8,1408]{1,0:T(8,128)S(1)} %add.9), channel_id=1, source_target_pairs={{0,2},{2,0},{4,6},{6,4},{8,10},{10,8},{12,14},{14,12},{1,3},{3,1},... | collective-permute-start | bytes 135176 | tf_op jit(solution)/shard_map/ppermute | solution.py:362
  37.9 5.8 %collective-permute-start.6 = (f32[8,128]{1,0:T(8,128)S(1)}, f32[8,128]{1,0:T(8,128)S(1)}, u32[]{:S(2)}, u32[]{:S(2)}) collective-permute-start(f32[8,128]{1,0:T(8,128)S(1)} %get-tuple-element.66.inner_ref), channel_id=1, source_target_pairs={{0,17},{1,16},{16,1},{17,0},{2,19},{3,18},{18,3},{19,2},{4,21},{5,... | collective-permute-start | bytes 12296 | tf_op jit(solution)/shard_map/ppermute | solution.py:34
  45.1 18.2 %collective-permute-start.12 = (bf16[4,704,128]{2,1,0:T(8,128)(2,1)S(1)}, bf16[4,704,128]{2,1,0:T(8,128)(2,1)S(1)}, u32[]{:S(2)}, u32[]{:S(2)}) collective-permute-start(bf16[4,704,128]{2,1,0:T(8,128)(2,1)S(1)} %shard_map.100.own_ref), channel_id=1, source_target_pairs={{0,17},{1,16},{16,1},{17,0},{2,19},{3,18},{18,3},{19,2},{4,21},{5,... | collective-permute-start | bytes 2162696 | tf_op jit(solution)/shard_map/ppermute | solution.py:34
  45.5 20.6 %collective-permute-start.15 = (bf16[128,1408]{1,0:T(8,128)(2,1)S(1)}, bf16[128,1408]{1,0:T(8,128)(2,1)S(1)}, u32[]{:S(2)}, u32[]{:S(2)}) collective-permute-start(bf16[128,1408]{1,0:T(8,128)(2,1)S(1)} %get-tuple-element.81.refs_0_), channel_id=1, source_target_pairs={{0,6},{2,4},{4,2},{6,0},{8,14},{10,12},{12,10},{14,8},{1,7},{3,5},... | collective-permute-start | bytes 1081352 | tf_op jit(solution)/shard_map/ppermute | solution.py:362
  48.1 18.0 %collective-permute-start.14 = (bf16[128,1408]{1,0:T(8,128)(2,1)S(1)}, bf16[128,1408]{1,0:T(8,128)(2,1)S(1)}, u32[]{:S(2)}, u32[]{:S(2)}) collective-permute-start(bf16[128,1408]{1,0:T(8,128)(2,1)S(1)} %get-tuple-element.81.refs_0_), channel_id=1, source_target_pairs={{0,4},{2,6},{4,0},{6,2},{8,12},{10,14},{12,8},{14,10},{1,5},{3,7},... | collective-permute-start | bytes 1081352 | tf_op jit(solution)/shard_map/ppermute | solution.py:362
  48.6 17.5 %collective-permute-start.13 = (bf16[128,1408]{1,0:T(8,128)(2,1)S(1)}, bf16[128,1408]{1,0:T(8,128)(2,1)S(1)}, u32[]{:S(2)}, u32[]{:S(2)}) collective-permute-start(bf16[128,1408]{1,0:T(8,128)(2,1)S(1)} %get-tuple-element.81.refs_0_), channel_id=1, source_target_pairs={{0,2},{2,0},{4,6},{6,4},{8,10},{10,8},{12,14},{14,12},{1,3},{3,1},... | collective-permute-start | bytes 1081352 | tf_op jit(solution)/shard_map/ppermute | solution.py:362
  49.0 17.1 %collective-permute-start.16 = (f32[8,1408]{1,0:T(8,128)S(1)}, f32[8,1408]{1,0:T(8,128)S(1)}, u32[]{:S(2)}, u32[]{:S(2)}) collective-permute-start(f32[8,1408]{1,0:T(8,128)S(1)} %add.10), channel_id=1, source_target_pairs={{0,4},{2,6},{4,0},{6,2},{8,12},{10,14},{12,8},{14,10},{1,5},{3,7},... | collective-permute-start | bytes 135176 | tf_op jit(solution)/shard_map/ppermute | solution.py:362
  67.5 2.8 %collective-permute-start.17 = (f32[352,768]{1,0:T(8,128)S(1)}, f32[352,768]{1,0:T(8,128)S(1)}, u32[]{:S(2)}, u32[]{:S(2)}) collective-permute-start(f32[352,768]{1,0:T(8,128)S(1)} %get-tuple-element.90), channel_id=1, source_target_pairs={{0,16},{16,0},{1,17},{17,1},{2,18},{18,2},{3,19},{19,3},{4,20},{20... | collective-permute-start | bytes 3244040 | tf_op jit(solution)/shard_map/ppermute | solution.py:30
  69.0 4.3 %collective-permute-start.18 = (f32[352,640]{1,0:T(8,128)S(1)}, f32[352,640]{1,0:T(8,128)S(1)}, u32[]{:S(2)}, u32[]{:S(2)}) collective-permute-start(f32[352,640]{1,0:T(8,128)S(1)} %get-tuple-element.93), channel_id=1, source_target_pairs={{0,16},{16,0},{1,17},{17,1},{2,18},{18,2},{3,19},{19,3},{4,20},{20... | collective-permute-start | bytes 2703368 | tf_op jit(solution)/shard_map/ppermute | solution.py:30
  70.4 5.9 %collective-permute-start.20 = (f32[128,1408]{1,0:T(8,128)S(1)}, f32[128,1408]{1,0:T(8,128)S(1)}, u32[]{:S(2)}, u32[]{:S(2)}) collective-permute-start(f32[128,1408]{1,0:T(8,128)S(1)} %get-tuple-element.96.total_ref), channel_id=1, source_target_pairs={{0,16},{16,0},{1,17},{17,1},{2,18},{18,2},{3,19},{19,3},{4,20},{20... | collective-permute-start | bytes 2162696 | tf_op jit(solution)/shard_map/ppermute | solution.py:30
  70.6 27.0 %collective-permute-start.22 = (bf16[176,768]{1,0:T(8,128)(2,1)S(1)}, bf16[176,768]{1,0:T(8,128)(2,1)S(1)}, u32[]{:S(2)}, u32[]{:S(2)}) collective-permute-start(bf16[176,768]{1,0:T(8,128)(2,1)S(1)} %get-tuple-element.91), channel_id=1, source_target_pairs={{0,8},{2,10},{4,12},{6,14},{8,0},{10,2},{12,4},{14,6},{1,9},{3,11}... | collective-permute-start | bytes 811016 | tf_op jit(solution)/shard_map/ppermute | solution.py:362
  73.4 23.8 %collective-permute-start.19 = (bf16[176,640]{1,0:T(8,128)(2,1)S(1)}, bf16[176,640]{1,0:T(8,128)(2,1)S(1)}, u32[]{:S(2)}, u32[]{:S(2)}) collective-permute-start(bf16[176,640]{1,0:T(8,128)(2,1)S(1)} %get-tuple-element.94), channel_id=1, source_target_pairs={{0,8},{2,10},{4,12},{6,14},{8,0},{10,2},{12,4},{14,6},{1,9},{3,11}... | collective-permute-start | bytes 675848 | tf_op jit(solution)/shard_map/ppermute | solution.py:362
  74.4 23.3 %collective-permute-start.21 = (f32[8,1408]{1,0:T(8,128)S(1)}, f32[8,1408]{1,0:T(8,128)S(1)}, u32[]{:S(2)}, u32[]{:S(2)}) collective-permute-start(f32[8,1408]{1,0:T(8,128)S(1)} %add.11.refs_0_), channel_id=1, source_target_pairs={{0,8},{2,10},{4,12},{6,14},{8,0},{10,2},{12,4},{14,6},{1,9},{3,11}... | collective-permute-start | bytes 135176 | tf_op jit(solution)/shard_map/ppermute | solution.py:362
